TPU v7x, 128 devices: a whole 4x4x4 slice. The times are simulated.
128 devices in a mesh: dp: 16 (over x_lo, z, core), ctx: 8 (over x_hi, y).
Axes of the slice: x: 4 (x_hi: 2, x_lo: 2; x = x_hi * 2 + x_lo), y: 4, z: 4, core: 2. Of those that a mesh axis runs over, the one named last changes fastest.
Arguments:
- hidden_rows: bfloat16 [16, 2048, 8192], P('dp', 'ctx'), may hold values from -6 to 6
- inner_rows: bfloat16 [16, 2048, 8192], P('dp', 'ctx'), may hold values from -6 to 6
- weight_proj: bfloat16 [8192, 320], P('dp'), may hold values from -0.03125 to 0.03125
- decay_log: float32 [64], replicated, as said below
- step_bias: float32 [64], replicated, may hold values from -0.5 to 0.5
- skip_gain: float32 [64], replicated, may hold values from 0.5 to 1.5
- grad_output: bfloat16 [16, 2048, 8192], P('dp', 'ctx'), may hold values from -6 to 6
Outputs:
- ssd_output: bfloat16 [16, 2048, 8192], P('dp', 'ctx')
- grad_inner: bfloat16 [16, 2048, 8192], P('dp', 'ctx')
- grad_hidden: bfloat16 [16, 2048, 8192], P('dp', 'ctx')
- grad_weight: float32 [8192, 320], P('dp')
Inputs may be any that keep to these rules, and one draw needn't show every extreme that they name: -exp(decay_log) is each head's decay rate per unit of step size.
All inputs are finite; a program needn't handle non-finite values.
Results may differ from a plain program's by a relative error of at most 0.005.
Values may be sent and summed in bfloat16 or wider, within the bound.
A program may use at most 384 MiB of HBM per device.

v0:
```python
from functools import partial

import jax
import jax.numpy as jnp
from jax import lax
from jax.sharding import PartitionSpec as P

P_SIZE = 128
N = 128
BLOCK = 128


highest = lax.Precision.HIGHEST


def prefix(part, axis, combine, identity, reverse):
    count = lax.axis_size(axis)
    place = lax.axis_index(axis)
    ahead = count - 1 - place if reverse else place
    gathered = jax.tree.map(lambda a: lax.all_gather(a, axis), part)
    state = jax.tree.map(lambda a, e: jnp.zeros_like(a) + jnp.asarray(e, a.dtype), part, identity)

    def one(step, state):
        source = count - 1 - step if reverse else step
        return combine(
            state, jax.tree.map(lambda a: lax.dynamic_index_in_dim(a, source, 0, False), gathered)
        )

    return lax.fori_loop(0, ahead, one, state)


def split_proj(projected, step_bias, decay_log):
    key_rows = projected[:, :N]
    query_rows = projected[:, N : 2 * N] * N ** (-0.5)
    step_sizes = jax.nn.softplus(projected[:, 2 * N :] + step_bias[None, :])
    log_decay = -jnp.exp(decay_log)[None, :] * step_sizes
    return (key_rows, query_rows, step_sizes, log_decay)


def block_step(skip_gain, carry_state, block):
    key_rows, query_rows, step_sizes, log_decay, value_rows = block
    block_len = key_rows.shape[0]
    values = value_rows.astype(jnp.float32).reshape(
        block_len, carry_state.shape[0], carry_state.shape[1]
    )
    running = jnp.cumsum(log_decay.T, axis=1)
    causal = jnp.arange(block_len)[:, None] >= jnp.arange(block_len)[None, :]
    log_gaps = running[:, :, None] - running[:, None, :]
    decays = jnp.where(causal[None], jnp.exp(jnp.where(causal[None], log_gaps, 0.0)), 0.0)
    scores = jnp.dot(query_rows, key_rows.T, precision=highest)
    mixing = decays * scores[None] * step_sizes.T[:, None, :]
    within = jnp.einsum("hts,shp->thp", mixing, values, precision=highest)
    carried = (
        jnp.einsum("tn,hpn->thp", query_rows, carry_state, precision=highest)
        * jnp.exp(running).T[:, :, None]
    )
    tail_weight = jnp.exp(running[:, -1:] - running) * step_sizes.T
    new_state = jnp.exp(running[:, -1])[:, None, None] * carry_state + jnp.einsum(
        "hs,shp,sn->hpn", tail_weight, values, key_rows, precision=highest
    )
    output = within + carried + skip_gain[None, :, None] * values
    return (new_state, output.reshape(block_len, -1))


def to_blocks(array, num_blocks):
    return array.reshape((num_blocks, -1) + array.shape[1:])


def run_blocks(projected, value_rows, state_start, decay_log, step_bias, skip_gain):
    key_rows, query_rows, step_sizes, log_decay = split_proj(projected, step_bias, decay_log)
    num_blocks = projected.shape[0] // BLOCK
    blocks = tuple(
        (
            to_blocks(item, num_blocks)
            for item in (key_rows, query_rows, step_sizes, log_decay, value_rows)
        )
    )
    final_state, outputs = lax.scan(partial(block_step, skip_gain), state_start, blocks)
    return (outputs.reshape(projected.shape[0], -1), final_state)


def combine_states(earlier, later_part):
    return (earlier[0] * later_part[0], later_part[0][:, None, None] * earlier[1] + later_part[1])


def shards(hidden_rows, inner_rows, weight_proj, decay_log, step_bias, skip_gain, grad_output):
    token_rows = hidden_rows.reshape(-1, hidden_rows.shape[-1])
    value_rows = inner_rows.reshape(-1, inner_rows.shape[-1])
    num_tokens = token_rows.shape[0]
    num_heads = decay_log.shape[0]
    cotangent = grad_output.reshape(num_tokens, num_heads, -1).astype(jnp.float32)
    slice_rows = token_rows
    projected = jnp.dot(
        slice_rows,
        lax.all_gather(weight_proj, "dp", axis=0, tiled=True),
        preferred_element_type=jnp.float32,
    )
    zero_state = jnp.zeros((num_heads, P_SIZE, N), jnp.float32)
    local_out, local_state = run_blocks(
        projected, value_rows, zero_state, decay_log, step_bias, skip_gain
    )
    key_rows, query_rows, step_sizes, log_decay = split_proj(projected, step_bias, decay_log)
    running = jnp.cumsum(log_decay, axis=0)
    decay_rows = jnp.exp(running)
    total_decay = jnp.exp(running[-1])
    identity = (jnp.ones((num_heads,), jnp.float32), jnp.zeros((num_heads, P_SIZE, N), jnp.float32))
    decay_before, state_in = prefix(
        (total_decay, local_state), "ctx", combine_states, identity, False
    )
    seed_grad = jnp.einsum(
        "thp,tn->hpn", cotangent * decay_rows[:, :, None], query_rows, precision=highest
    )
    decay_after, later_grad = prefix(
        (total_decay, seed_grad), "ctx", combine_states, identity, True
    )

    def full_pass(proj_in, values_in, state_start):
        return run_blocks(proj_in, values_in, state_start, decay_log, step_bias, skip_gain)

    recomputed, pullback = jax.vjp(full_pass, projected, value_rows, state_in)
    ssd_output = recomputed[0].astype(jnp.bfloat16).reshape(inner_rows.shape)
    grad_proj, grad_values, grad_state = pullback((cotangent.reshape(num_tokens, -1), later_grad))
    grad_inner = grad_values.reshape(inner_rows.shape)
    grad_low = grad_proj.astype(jnp.bfloat16)
    grad_tokens = lax.dot_general(
        grad_low,
        lax.all_gather(weight_proj, "dp", axis=0, tiled=True),
        (((1,), (1,)), ((), ())),
        preferred_element_type=jnp.float32,
    )
    grad_hidden = grad_tokens.astype(jnp.bfloat16).reshape(hidden_rows.shape)
    slice_rows = token_rows
    grad_shard = lax.psum_scatter(
        lax.dot_general(
            slice_rows, grad_low, (((0,), (0,)), ((), ())), preferred_element_type=jnp.float32
        ),
        "dp",
        scatter_dimension=0,
        tiled=True,
    )
    grad_weight = lax.psum(grad_shard, "ctx")
    return (ssd_output, grad_inner, grad_hidden, grad_weight)


def solution(mesh):
    placed = (
        P("dp", "ctx", None),
        P("dp", "ctx", None),
        P("dp", None),
        P(),
        P(),
        P(),
        P("dp", "ctx", None),
    )
    return jax.shard_map(
        shards,
        mesh=mesh,
        in_specs=placed,
        out_specs=(P("dp", "ctx", None), P("dp", "ctx", None), P("dp", "ctx", None), P("dp", None)),
        check_vma=False,
    )
```

profile of v0, /device:TPU:0, one launch (start us, length us, event | category | flops | bytes accessed | tf_op | source)
XLA Modules:
  0.0 1180.2 jit_solution(5382419175073532201)
XLA Ops:
  8.0 6.3 copy.156
  14.3 37.3 %all-gather.7.cloned.1.call-done = bf16[8192,320]{0,1:T(8,128)(2,1)} async-done(((bf16[512,320]{0,1:T(8,128)(2,1)}), bf16[8192,320]{0,1:T(8,128)(2,1)}) %all-gather.7.cloned.1.call-update) | async-done | bytes 5242896 | tf_op jit(solution)/shard_map/all_gather | solution.py:95
  57.2 16.2 %while.120 = (s32[]{:T(128)}, f32[64,128,128]{2,1,0:T(8,128)}, f32[2,128,64]{1,2,0:T(8,128)S(1)}, f32[2,128,64]{1,2,0:T(8,128)S(1)}, bf16[2,128,8192]{1,2,0:T(8,...) while((s32[]{:T(128)}, f32[64,128,128]{2,1,0:T(8,128)}, ...), condition=%wide.region_4.5_spmd.clone, body=%wide.region_2.4_spmd.clone.sunk | while | flops 1616912384 | bytes 15009659 | solution.py:78
  66.8 6.5 fusion.209
  73.5 7.0 copy.192
  81.4 11.2 fusion.115
  92.9 6.4 convert_element_type.84
  99.6 22.8 %all-gather.2 = f32[8,1,64]{2,1,0:T(1,128)S(1)} all-gather(f32[1,1,64]{2,1,0:T(1,128)S(1)} %bitcast.533), channel_id=1, replica_groups=mesh['dp'=16,'ctx'=8] {'ctx'}, dimensions={0}, use_global_device_ids=true | all-gather | bytes 2304 | tf_op jit(solution)/shard_map/all_gather | solution.py:20
  122.4 285.1 %all-gather.9.cloned.1.call-done = f32[512,128,128]{2,1,0:T(8,128)} async-done(((f32[64,128,128]{2,1,0:T(8,128)}), f32[512,128,128]{2,1,0:T(8,128)}) %all-gather.9.cloned.1.call-update) | async-done | bytes 33554448 | tf_op jit(solution)/shard_map/all_gather | solution.py:20
  410.7 90.3 %while.118 = (s32[]{:T(128)}, f32[64,128,128]{2,1,0:T(8,128)}, bf16[2,128,8192]{1,2,0:T(8,128)(2,1)}, f32[2,64,128,128]{3,2,1,0:T(8,128)}, f32[2,128,128]{1,2,0:...) while((s32[]{:T(128)}, f32[64,128,128]{2,1,0:T(8,128)}, ...), condition=%wide.region_9.10_spmd.clone.clone, body=%wide.region_7.9_spmd.clone.clone.sunk | while | flops 4882202624 | bytes 364389344 | solution.py:78
  411.6 9.5 multiply_dynamic-update-slice_fusion.2
  421.2 5.7 bitcast_dynamic-update-slice_fusion.18
  430.3 6.2 fusion.179
  441.8 5.9 bitcast_dynamic-update-slice_fusion.22
  447.8 8.4 multiply_add_fusion.4
  457.7 7.7 multiply_dynamic-update-slice_fusion.2
  474.5 6.2 fusion.179
  486.0 5.9 bitcast_dynamic-update-slice_fusion.22
  491.9 8.4 multiply_add_fusion.4
  501.0 241.4 %all-gather.11.cloned.1.call-done = f32[512,128,128]{2,1,0:T(8,128)} async-done(((f32[64,128,128]{2,1,0:T(8,128)}), f32[512,128,128]{2,1,0:T(8,128)}) %all-gather.11.cloned.1.call-update) | async-done | bytes 33554448 | tf_op jit(solution)/shard_map/all_gather | solution.py:20
  744.9 41.7 %while.117 = (s32[]{:T(128)}, f32[64,128,128]{2,1,0:T(8,128)}, s32[]{:T(128)}, f32[8,64]{1,0:T(8,128)S(1)}, f32[8,64,128,128]{3,2,1,0:T(8,128)}, /*index=5*/s32[]{:T(128)}, s32[]{:T(128)}, s32[]{:T(128)}, s32[]{:T(128)}) while((s32[]{:T(128)}, f32[64,128,128]{2,1,0:T(8,128)}, s32[]{:T(128)}, f32[8,64]{1,0:T(8,128)S(1)}, ...), condition=%wide.region_11.12_spmd, body=%wide.region_10.11_spmd.sunk | while | flops 2097158 | bytes 12583827 | solution.py:29
  744.9 6.0 bitcast_add_fusion.7
  750.9 5.9 bitcast_add_fusion.7
  756.9 5.9 bitcast_add_fusion.7
  762.8 5.9 bitcast_add_fusion.7
  768.8 5.9 bitcast_add_fusion.7
  774.7 5.9 bitcast_add_fusion.7
  780.7 5.9 bitcast_add_fusion.7
  789.2 210.7 %while.119 = (s32[]{:T(128)}, f32[64,128,128]{2,1,0:T(8,128)}, f32[2,128,128]{2,1,0:T(8,128)S(1)}, f32[2,128,128]{2,1,0:T(8,128)S(1)}, f32[2,128,64]{2,1,0:T(8,1...) while((s32[]{:T(128)}, f32[64,128,128]{2,1,0:T(8,128)}, ...), condition=%wide.region_21.22_spmd.clone.clone, body=%wide.region_12.21_spmd.clone.clone.sunk | while | flops 9741361152 | bytes 212262384 | solution.py:78
  810.8 7.4 fusion.200
  826.1 11.1 fusion.206
  843.2 5.6 copy.243
  848.8 13.5 %fusion.196 = (f32[64,128]{1,0:T(8,128)S(1)}, f32[64,128]{1,0:T(8,128)S(1)}, f32[128,128]{1,0:T(8,128)S(1)}, f32[64,128]{1,0:T(8,128)S(1)}) fusion(f32[2,64,128,128]{3,2,1,0:T(8,128)} %get-tuple-element.2707, s32[]{:T(128)S(6)} %sub.230, f32[128,128]{1,0:T(8,128)S(1)} %dynamic-slice_bitcast_fusion.22, ...), kind=kOutput, calls=%fused_computation.44.clone.1 | convolution fusion | flops 1622106112 | bytes 21251072 | tf_op jit(solution)/shard_map/transpose(jvp())/while/body/eval_jaxpr/hts,shp->thp/dot_general | solution.py:52
  875.8 10.1 fusion.198
  886.3 10.3 fusion.195
  896.6 6.5 multiply_add_fusion.5
  903.5 7.4 fusion.200
  918.8 11.1 fusion.206
  935.9 5.6 copy.243
  941.5 13.5 %fusion.196 = (f32[64,128]{1,0:T(8,128)S(1)}, f32[64,128]{1,0:T(8,128)S(1)}, f32[128,128]{1,0:T(8,128)S(1)}, f32[64,128]{1,0:T(8,128)S(1)}) fusion(f32[2,64,128,128]{3,2,1,0:T(8,128)} %get-tuple-element.2707, s32[]{:T(128)S(6)} %sub.230, f32[128,128]{1,0:T(8,128)S(1)} %dynamic-slice_bitcast_fusion.22, ...), kind=kOutput, calls=%fused_computation.44.clone.1 | convolution fusion | flops 1622106112 | bytes 21251072 | tf_op jit(solution)/shard_map/transpose(jvp())/while/body/eval_jaxpr/hts,shp->thp/dot_general | solution.py:52
  968.4 10.1 fusion.198
  978.9 10.3 fusion.195
  989.3 6.5 multiply_add_fusion.5
  1001.3 7.7 convolution_bitcast_fusion
  1009.1 75.2 %reduce-scatter.2.cloned.1.call-done = f32[512,320]{0,1:T(8,128)} async-done(((f32[8192,320]{0,1:T(8,128)}), f32[512,320]{0,1:T(8,128)}) %reduce-scatter.2.cloned.1.call-update) | async-done | bytes 655376 | tf_op jit(solution)/shard_map/reduce_scatter | solution.py:133
  1084.3 6.3 copy.164
  1090.7 6.9 fusion.114
  1097.5 74.0 %all-reduce.7.cloned.1.call-done = f32[512,320]{0,1:T(8,128)} async-done(((f32[512,320]{0,1:T(8,128)}), f32[512,320]{0,1:T(8,128)}) %all-reduce.7.cloned.1.call-update) | async-done | bytes 655376 | tf_op jit(solution)/shard_map/psum | solution.py:141
  (290 shorter events, 110.6 us)
Async XLA Ops:
  7.2 44.4 %all-gather.7.cloned.1.call-start = ((), (), s32[]{:S(2)}) async-start(), calls=%async_computation.1 | async-start | bytes 5570560 | tf_op jit(solution)/shard_map/all_gather | solution.py:95
  7.9 399.6 %all-gather.9.cloned.1.call-start = ((), (), s32[]{:S(2)}) async-start(), calls=%async_computation.4 | async-start | bytes 37748736 | tf_op jit(solution)/shard_map/all_gather | solution.py:20
  8.0 6.3 copy-start.23
  14.3 42.7 %copy-start.21 = (f32[64]{0:T(128)}, f32[64]{0:T(128)S(1)}, u32[]{:S(2)}) copy-start(f32[64]{0:T(128)S(1)} %exponential_negate_fusion) | copy-start | bytes 772
  14.3 42.7 %copy-start.19 = (f32[64]{0:T(128)S(1)}, f32[64]{0:T(128)}, u32[]{:S(2)}) copy-start(f32[64]{0:T(128)} %param.21) | copy-start | bytes 772
  56.9 24.5 %copy-start.12 = (f32[256,320]{0,1:T(8,128)}, f32[256,320]{0,1:T(8,128)S(1)}, u32[]{:S(2)}) copy-start(f32[256,320]{0,1:T(8,128)S(1)} %fusion.118) | copy-start | bytes 983044
  73.4 669.0 %all-gather.11.cloned.1.call-start = ((), (), s32[]{:S(2)}) async-start(), calls=%async_computation.5 | async-start | bytes 37748736 | tf_op jit(solution)/shard_map/all_gather | solution.py:20
  92.6 991.7 %reduce-scatter.2.cloned.1.call-start = ((), (), s32[]{:S(2)}) async-start(), calls=%async_computation.2 | async-start | bytes 11141120 | tf_op jit(solution)/shard_map/reduce_scatter | solution.py:133
  411.3 9.9 slice-start.4
  411.6 9.7 slice-start.5
  421.2 8.9 copy-start.4
  421.2 17.7 %slice-start.6 = ((s8[8388608]{0:T(1024)(128)(4,1)}), s8[4194304]{0:T(1024)(128)(4,1)S(1)}, s32[]{:S(2)}) async-start(s8[8388608]{0:T(1024)(128)(4,1)} %bitcast.511), calls=%async_computation.12 | async-start | bytes 8388608 | tf_op jit(solution)/shard_map/jvp()/while
  430.2 6.4 copy-start.10
  430.3 8.7 slice-start.2
  430.3 8.7 slice-start.3
  430.3 8.6 slice-start.7
  440.9 6.8 copy-start.3
  440.9 15.3 %copy-start.7 = (f32[2,128,64,128]{1,3,2,0:T(8,128)}, f32[2,128,64,128]{1,3,2,0:T(8,128)S(1)}, u32[]{:S(2)}) copy-start(f32[2,128,64,128]{1,3,2,0:T(8,128)S(1)} %get-tuple-element.2578) | copy-start | bytes 25165828 | tf_op jit(solution)/shard_map/jvp()/while
  447.7 8.4 copy-start.2
  457.5 8.0 slice-start.4
  457.7 7.8 slice-start.5
  465.5 8.8 copy-start.4
  465.5 17.6 %slice-start.6 = ((s8[8388608]{0:T(1024)(128)(4,1)}), s8[4194304]{0:T(1024)(128)(4,1)S(1)}, s32[]{:S(2)}) async-start(s8[8388608]{0:T(1024)(128)(4,1)} %bitcast.511), calls=%async_computation.12 | async-start | bytes 8388608 | tf_op jit(solution)/shard_map/jvp()/while
  474.3 6.4 copy-start.10
  474.4 8.7 slice-start.2
  474.4 8.7 slice-start.3
  474.4 8.7 slice-start.7
  485.0 6.8 copy-start.3
  485.0 15.2 %copy-start.7 = (f32[2,128,64,128]{1,3,2,0:T(8,128)}, f32[2,128,64,128]{1,3,2,0:T(8,128)S(1)}, u32[]{:S(2)}) copy-start(f32[2,128,64,128]{1,3,2,0:T(8,128)S(1)} %get-tuple-element.2578) | copy-start | bytes 25165828 | tf_op jit(solution)/shard_map/jvp()/while
  491.9 8.4 copy-start.2
  501.0 243.9 %copy-start.14 = (f32[2,128,64,1]{1,2,3,0:T(8,128)}, f32[2,128,64,1]{1,2,3,0:T(8,128)S(1)}, u32[]{:S(2)}) copy-start(f32[2,128,64,1]{1,2,3,0:T(8,128)S(1)} %get-tuple-element.2625) | copy-start | bytes 196612
  501.0 243.9 %copy-start.17 = (f32[2,64]{1,0:T(2,128)}, f32[2,64]{1,0:T(2,128)S(1)}, u32[]{:S(2)}) copy-start(f32[2,64]{1,0:T(2,128)S(1)} %get-tuple-element.2636) | copy-start | bytes 1540
  501.0 243.9 %copy-start.24 = (f32[2,64,1,1]{1,3,2,0:T(1,128)}, f32[2,64,1,1]{1,3,2,0:T(1,128)S(1)}, u32[]{:S(2)}) copy-start(f32[2,64,1,1]{1,3,2,0:T(1,128)S(1)} %get-tuple-element.2623) | copy-start | bytes 1540
  789.2 211.1 %copy-start.20 = (f32[64]{0:T(128)S(1)}, f32[64]{0:T(128)}, u32[]{:S(2)}) copy-start(f32[64]{0:T(128)} %param.21) | copy-start | bytes 772
  789.2 211.1 %copy-start.22 = (f32[64]{0:T(128)S(1)}, f32[64]{0:T(128)}, u32[]{:S(2)}) copy-start(f32[64]{0:T(128)} %copy-done.21) | copy-start | bytes 772
  810.8 7.4 copy-start.8
  810.8 7.4 copy-start.5
  875.8 10.1 copy-start
  875.8 10.1 copy-start.13
  886.2 10.4 copy-start.1
  886.3 10.4 copy-start.9
  903.5 7.4 copy-start.8
  903.5 7.4 copy-start.5
  968.4 10.1 copy-start
  968.4 10.1 copy-start.13
  978.9 10.4 copy-start.1
  978.9 10.4 copy-start.9
  1009.0 162.5 %all-reduce.7.cloned.1.call-start = ((), (), s32[]{:S(2)}) async-start(), calls=%async_computation.3 | async-start | bytes 1310720 | tf_op jit(solution)/shard_map/psum | solution.py:141
  (12 other events, 33.7 us)
Sparse Core Ops, SparseCore 0:
  9.7 41.8 all-gather.6
  73.5 333.9 all-gather.8
  410.4 331.8 all-gather.10
  1009.1 75.1 reduce-scatter.1
  1086.6 84.8 all-reduce.6
where the time goes:
time: 1190 us; the launch traced here: 1180 us
  waiting for transfers between devices  714 us (60%)
  matrix products  202 us (17%)
  local copies, waits for them, and re-layouts  102 us (9%)
  other arithmetic  97.5 us (8%)
  loops' own time  26.9 us (2%)
  blocking collectives  22.8 us (2%)
  between operations  14.4 us (1%)
    all_gather x2, waiting for transfers between devices, prefix(): gathered = jax.tree.map(lambda a: lax.all_gather(a, axis), part)  526 us
    reduce_scatter x1, waiting for transfers between devices, shards(): lax.psum_scatter(lax.dot_general(slice_rows, grad_low, (((0,), (0,)), (()...  75.2 us
    psum x1, waiting for transfers between devices, shards(): grad_weight = lax.psum(grad_shard, 'ctx')  74 us
    dot_general x8, matrix products, block_step(): jnp.einsum('hs,shp,sn->hpn', tail_weight, values, key_rows, precision=hig...  63.7 us
    dot_general x6, matrix products, block_step(): within = jnp.einsum('hts,shp->thp', mixing, values, precision=highest)  61.6 us
    dot_general x6, matrix products, block_step(): jnp.einsum('tn,hpn->thp', query_rows, carry_state, precision=highest)  44.3 us
    add x7, other arithmetic, combine_states(): later_part[0][:, None, None] * earlier[1] + later_part[1]  41.6 us
    all_gather x1, waiting for transfers between devices, shards(): lax.all_gather(weight_proj, 'dp', axis=0, tiled=True)  37.3 us
  transfers between devices with their start and end apart: 5, of which 5 were waited for; matrix products, arithmetic and copies ran while one was open for 11% of the time, Pallas kernels for 0%

commit v1 on v0

v1 whole, which is shorter than its diff:
```python
from functools import partial

import jax
import jax.numpy as jnp
from jax import lax
from jax.experimental import pallas as pl
from jax.experimental.pallas import tpu as pltpu
from jax.sharding import PartitionSpec as P

PS = 128
NS = 128
CHUNK = 2
LAG = 2
MESH = pl.DeviceIdType.MESH
highest = lax.Precision.HIGHEST
f32 = jnp.float32
bf16 = jnp.bfloat16
NN = (((1,), (0,)), ((), ()))
NT = (((1,), (1,)), ((), ()))
TN = (((0,), (0,)), ((), ()))


def dot(a, b, dims=NN):
    return lax.dot_general(a, b, dims, preferred_element_type=f32)


def dot_high(a, b, dims=NN):
    return lax.dot_general(a, b, dims, preferred_element_type=f32, precision=highest)


def split(a):
    high = a.astype(bf16)
    return high, (a - high.astype(f32)).astype(bf16)


def scan_kernel(
    pieces, heads, gain_ref, proj_ref, head_ref, x_ref, dy_ref, y_ref, dx_ref, grad_ref,
    run, run_t, step_t, step_c, key_t, query_t, key_hl, query_hl, scores,
    acc_diff, acc_cross, acc_const, dq, dk, dscores,
    state_in, state_out, grad_in, grad_out, sf, rf, sb, rb,
):
    k = lax.axis_index("ctx")
    last = pieces - 1
    tokens = proj_ref.shape[0]
    half = tokens // 2
    chunks = heads // CHUNK
    right = lax.rem(k + 1, pieces)
    left = lax.rem(k + pieces - 1, pieces)

    barrier = pltpu.get_barrier_semaphore()
    for neighbour in (left, right):
        pl.semaphore_signal(barrier, inc=1, device_id={"ctx": neighbour}, device_id_type=MESH)

    rows = lax.broadcasted_iota(jnp.int32, (tokens, tokens), 0)
    cols = lax.broadcasted_iota(jnp.int32, (tokens, tokens), 1)
    key = proj_ref[:, :NS]
    query = proj_ref[:, NS : 2 * NS] * NS ** (-0.5)
    bias = head_ref[0:1, :]
    rate = jnp.exp(head_ref[1:2, :])
    pre = proj_ref[:, 2 * NS :] + bias
    steps = jnp.maximum(pre, 0.0) + jnp.log1p(jnp.exp(-jnp.abs(pre)))
    running = dot_high((rows >= cols).astype(f32), -rate * steps)
    run[...] = running
    run_t[...] = running.T
    step_c[...] = steps
    step_t[...] = steps.T
    key_t[...] = key.T
    query_t[...] = query.T
    high, low = split(key)
    key_hl[:, :NS] = high
    key_hl[:, NS:] = low
    high, low = split(query)
    query_hl[:, :NS] = high
    query_hl[:, NS:] = low
    scores[...] = dot_high(query, key, NT)
    dq[...] = jnp.zeros_like(dq)
    dk[...] = jnp.zeros_like(dk)
    dscores[...] = jnp.zeros_like(dscores)
    acc_diff[...] = jnp.zeros_like(acc_diff)
    acc_cross[...] = jnp.zeros_like(acc_cross)
    acc_const[...] = jnp.zeros_like(acc_const)

    @pl.when(k == 0)
    def _():
        state_in[...] = jnp.zeros_like(state_in)

    @pl.when(k == last)
    def _():
        grad_in[...] = jnp.zeros_like(grad_in)

    pl.semaphore_wait(barrier, 2)

    def copy_fwd(j):
        part = pl.ds(j * CHUNK, CHUNK)
        return pltpu.make_async_remote_copy(
            src_ref=state_out.at[part], dst_ref=state_in.at[part],
            send_sem=sf.at[j], recv_sem=rf.at[j],
            device_id={"ctx": right}, device_id_type=MESH,
        )

    def copy_bwd(j):
        part = pl.ds(j * CHUNK, CHUNK)
        return pltpu.make_async_remote_copy(
            src_ref=grad_out.at[part], dst_ref=grad_in.at[part],
            send_sem=sb.at[j], recv_sem=rb.at[j],
            device_id={"ctx": left}, device_id_type=MESH,
        )

    def columns(h):
        return pl.ds(pl.multiple_of(h * PS, PS), PS)

    def forward(j):
        local = []
        for u in range(CHUNK):
            h = j * CHUNK + u
            r_row = run_t[pl.ds(h, 1), :]
            r_end = r_row[:, tokens - 1 : tokens]
            weight = jnp.exp(r_end - r_row) * step_t[pl.ds(h, 1), :]
            high, low = split(key_t[...] * weight)
            x = x_ref[:, columns(h)]
            local.append((h, jnp.exp(r_end), dot(high, x) + dot(low, x)))

        @pl.when(k > 0)
        def _():
            copy_fwd(j).wait_recv()

        @pl.when(k < last)
        def _():
            for h, decay, state in local:
                state_out[h] = (decay * state_in[h].astype(f32) + state).astype(bf16)
            copy_fwd(j).start()

    def backward(j):
        local = []
        for u in range(CHUNK):
            h = j * CHUNK + u
            r_row = run_t[pl.ds(h, 1), :]
            r_end = r_row[:, tokens - 1 : tokens]
            high, low = split(query_t[...] * jnp.exp(r_row))
            dy = dy_ref[:, columns(h)]
            local.append((h, jnp.exp(r_end), dot(high, dy) + dot(low, dy)))

        @pl.when(k < last)
        def _():
            copy_bwd(j).wait_recv()

        @pl.when(k > 0)
        def _():
            for h, decay, state in local:
                grad_out[h] = (decay * grad_in[h].astype(f32) + state).astype(bf16)
            copy_bwd(j).start()

    def compute(h):
        lane = lax.broadcasted_iota(jnp.int32, (tokens, NS), 1)
        mine = lane == h
        r_col = jnp.sum(jnp.where(mine, run[...], 0.0), axis=1, keepdims=True)
        s_col = jnp.sum(jnp.where(mine, step_c[...], 0.0), axis=1, keepdims=True)
        r_row = run_t[pl.ds(h, 1), :]
        s_row = step_t[pl.ds(h, 1), :]
        r_end = r_row[:, tokens - 1 : tokens]
        x = x_ref[:, columns(h)]
        dy = dy_ref[:, columns(h)]
        gain = gain_ref[h]

        def decays(begin, width):
            t = lax.broadcasted_iota(jnp.int32, (half, width), 0) + begin
            s = lax.broadcasted_iota(jnp.int32, (half, width), 1)
            gaps = r_col[begin : begin + half] - r_row[:, :width]
            return jnp.exp(jnp.where(t >= s, gaps, -1e30)) * s_row[:, :width]

        top = decays(0, half)
        bottom = decays(half, tokens)
        mix_top = (top * scores[:half, :half]).astype(bf16)
        mix_bottom = (bottom * scores[half:, :]).astype(bf16)
        dscores[:half, :half] += top * dot(dy[:half], x[:half], NT)
        dscores[half:, :] += bottom * dot(dy[half:], x, NT)
        y = jnp.concatenate([dot(mix_top, x[:half]), dot(mix_bottom, x)], axis=0)
        dx = dot(mix_bottom, dy[half:], TN)
        dx = jnp.concatenate([dx[:half] + dot(mix_top, dy[:half], TN), dx[half:]], axis=0)

        state = state_in[h]
        grad = grad_in[h]
        from_start = jnp.exp(r_col)
        to_end = jnp.exp(r_end - r_col) * s_col
        y += from_start * dot(query_hl[...], jnp.concatenate([state, state], axis=0))
        carried = to_end * dot(key_hl[...], jnp.concatenate([grad, grad], axis=0))
        dx += carried
        dq[...] += from_start * dot(dy, state, NT)
        dk[...] += to_end * dot(x, grad, NT)
        xf = x.astype(f32)
        dyf = dy.astype(f32)
        y_ref[:, columns(h)] = (y + gain * xf).astype(bf16)
        dx_ref[:, columns(h)] = (dx + gain * dyf).astype(bf16)
        cross = xf * dx
        acc_cross[...] = jnp.where(mine, jnp.sum(cross, axis=1, keepdims=True), acc_cross[...])
        acc_diff[...] = jnp.where(
            mine, jnp.sum(dyf * y - cross, axis=1, keepdims=True), acc_diff[...]
        )
        inner = jnp.sum(grad.astype(f32) * state.astype(f32), axis=0, keepdims=True)
        inner = jnp.sum(inner, axis=1, keepdims=True)
        outer = jnp.sum(jnp.sum(xf * carried, axis=0, keepdims=True), axis=1, keepdims=True)
        const = jnp.exp(r_end) * inner + outer
        acc_const[...] = jnp.where(mine[:8], const, acc_const[...])

    start_f = LAG * k
    start_b = LAG * (last - k)
    start_c = jnp.maximum(start_f, start_b)

    def iteration(i, carry):
        jf = i - start_f
        jb = i - start_b
        jc = i - start_c

        @pl.when((jf >= 0) & (jf < chunks))
        def _():
            forward(jf)

        @pl.when((jb >= 0) & (jb < chunks))
        def _():
            backward(jb)

        @pl.when((jc >= 0) & (jc < chunks))
        def _():
            for u in range(CHUNK):
                compute(jc * CHUNK + u)

        return carry

    lax.fori_loop(0, chunks + LAG * last, iteration, 0)

    @pl.when(k < last)
    def _():
        def wait(j, carry):
            copy_fwd(j).wait_send()
            return carry

        lax.fori_loop(0, chunks, wait, 0)

    @pl.when(k > 0)
    def _():
        def wait(j, carry):
            copy_bwd(j).wait_send()
            return carry

        lax.fori_loop(0, chunks, wait, 0)

    key = proj_ref[:, :NS]
    query = proj_ref[:, NS : 2 * NS] * NS ** (-0.5)
    pre = proj_ref[:, 2 * NS :] + head_ref[0:1, :]
    d_log = dot_high((cols >= rows).astype(f32), acc_diff[...]) + acc_const[0:1, :]
    slope = 1.0 / (1.0 + jnp.exp(-pre))
    ratio = jnp.where(pre < -20.0, 1.0, slope / step_c[...])
    dk_all = dk[...] + dot_high(dscores[...].T, query)
    dq_all = dq[...] + dot_high(dscores[...], key)
    grad_ref[:, :NS] = dk_all.astype(bf16)
    grad_ref[:, NS : 2 * NS] = (dq_all * NS ** (-0.5)).astype(bf16)
    rate = jnp.exp(head_ref[1:2, :])
    grad_ref[:, 2 * NS :] = (acc_cross[...] * ratio - rate * d_log * slope).astype(bf16)


def scan_pass(pieces, gain, proj, head, x, dy):
    tokens, width = x.shape
    heads = width // PS
    chunks = heads // CHUNK
    vm = pl.BlockSpec(memory_space=pltpu.VMEM)
    big = (heads, NS, PS)
    return pl.pallas_call(
        partial(scan_kernel, pieces, heads),
        out_shape=(
            jax.ShapeDtypeStruct(x.shape, bf16),
            jax.ShapeDtypeStruct(x.shape, bf16),
            jax.ShapeDtypeStruct((tokens, 3 * NS), bf16),
        ),
        in_specs=[pl.BlockSpec(memory_space=pltpu.SMEM), vm, vm, vm, vm],
        out_specs=(vm, vm, vm),
        scratch_shapes=[
            pltpu.VMEM((tokens, NS), f32),
            pltpu.VMEM((NS, tokens), f32),
            pltpu.VMEM((NS, tokens), f32),
            pltpu.VMEM((tokens, NS), f32),
            pltpu.VMEM((NS, tokens), f32),
            pltpu.VMEM((NS, tokens), f32),
            pltpu.VMEM((tokens, 2 * NS), bf16),
            pltpu.VMEM((tokens, 2 * NS), bf16),
            pltpu.VMEM((tokens, tokens), f32),
            pltpu.VMEM((tokens, NS), f32),
            pltpu.VMEM((tokens, NS), f32),
            pltpu.VMEM((8, NS), f32),
            pltpu.VMEM((tokens, NS), f32),
            pltpu.VMEM((tokens, NS), f32),
            pltpu.VMEM((tokens, tokens), f32),
            pltpu.VMEM(big, bf16),
            pltpu.VMEM(big, bf16),
            pltpu.VMEM(big, bf16),
            pltpu.VMEM(big, bf16),
            pltpu.SemaphoreType.DMA((chunks,)),
            pltpu.SemaphoreType.DMA((chunks,)),
            pltpu.SemaphoreType.DMA((chunks,)),
            pltpu.SemaphoreType.DMA((chunks,)),
        ],
        compiler_params=pltpu.CompilerParams(
            collective_id=0, has_side_effects=True, vmem_limit_bytes=48 * 2**20
        ),
    )(gain, proj, head, x, dy)


def shards(pieces, hidden_rows, inner_rows, weight_proj, decay_log, step_bias, skip_gain, grad_output):
    token_rows = hidden_rows.reshape(-1, hidden_rows.shape[-1])
    value_rows = inner_rows.reshape(-1, inner_rows.shape[-1])
    cotangent = grad_output.reshape(value_rows.shape)
    cols = weight_proj.shape[1]
    heads = decay_log.shape[0]
    whole = lax.all_gather(weight_proj, "dp", axis=0, tiled=True)
    padded = jnp.pad(whole, ((0, 0), (0, 3 * NS - cols)))
    projected = jnp.dot(token_rows, padded, preferred_element_type=f32)
    head = jnp.pad(jnp.stack([step_bias, decay_log]), ((0, 6), (0, NS - heads)))
    output, grad_values, grad_low = scan_pass(
        pieces, skip_gain, projected, head, value_rows, cotangent
    )
    ssd_output = output.reshape(inner_rows.shape)
    grad_inner = grad_values.reshape(inner_rows.shape)
    grad_low = grad_low[:, :cols]
    grad_tokens = dot(grad_low, whole, NT)
    grad_hidden = grad_tokens.astype(bf16).reshape(hidden_rows.shape)
    grad_shard = lax.psum_scatter(
        dot(token_rows, grad_low, TN), "dp", scatter_dimension=0, tiled=True
    )
    grad_weight = lax.psum(grad_shard, "ctx")
    return (ssd_output, grad_inner, grad_hidden, grad_weight)


def solution(mesh):
    rows = P("dp", "ctx", None)
    return jax.shard_map(
        partial(shards, mesh.shape["ctx"]),
        mesh=mesh,
        in_specs=(rows, rows, P("dp", None), P(), P(), P(), rows),
        out_specs=(rows, rows, rows, P("dp", None)),
        check_vma=False,
    )
```

time: 1190 us -> 359 us (0.30)
  waiting for transfers between devices: 714 us -> 201 us
  matrix products: 202 us -> 18.5 us
  Pallas kernels: 0 us -> 114 us
  other arithmetic: 97.5 us -> 0.68 us
  local copies, waits for them, and re-layouts: 102 us -> 9.66 us
  loops' own time: 26.9 us -> 0 us
  blocking collectives: 22.8 us -> 0 us
    all_gather x3 -> x1, waiting for transfers between devices: 564 us -> 42.9 us  [shards(): whole = lax.all_gather(weight_proj, 'dp', axis=0, tiled=True)]
    dot_general x30 -> x3, matrix products: 202 us -> 18.5 us  [the longest x2 12.4 us: dot(): return lax.dot_general(a, b, dims, preferred_element_type=f32)]
    pallas_call x0 -> x1, Pallas kernels: none -> 114 us  [scan_pass(): pl.pallas_call(partial(scan_kernel, pieces, heads), out_shape=(jax.ShapeD...]
    add x7 -> x0, other arithmetic: 41.6 us -> none  [combine_states(): later_part[0][:, None, None] * earlier[1] + later_part[1]]
    another operation x5 -> x0, loops' own time: 26.9 us -> none  [the longest x3 26.5 us: run_blocks(): lax.scan(partial(block_step, skip_gain), state_start, blocks)]
    dynamic_update_slice x20 -> x0, local copies, waits for them, and re-layouts: 26 us -> none  [run_blocks(): lax.scan(partial(block_step, skip_gain), state_start, blocks)]
    all_gather x1 -> x0, blocking collectives: 22.8 us -> none  [prefix(): gathered = jax.tree.map(lambda a: lax.all_gather(a, axis), part)]
    dynamic_update_slice x8 -> x0, other arithmetic: 21.2 us -> none  [run_blocks(): lax.scan(partial(block_step, skip_gain), state_start, blocks)]
  transfers between devices with their start and end apart: 5 -> 3, of which waited for: 5 -> 3; matrix products, arithmetic and copies ran while one was open for 11% -> 2% of each run, Pallas kernels for 0% -> 0%
where the time goes in v1:
time: 359 us; the launch traced here: 358 us
  waiting for transfers between devices  201 us (56%)
  Pallas kernels  114 us (32%)
  matrix products  18.5 us (5%)
  between operations  13.8 us (4%)
  local copies, waits for them, and re-layouts  9.66 us (3%)
    pallas_call x1, Pallas kernels, scan_pass(): pl.pallas_call(partial(scan_kernel, pieces, heads), out_shape=(jax.ShapeD...  114 us
    psum x1, waiting for transfers between devices, shards(): grad_weight = lax.psum(grad_shard, 'ctx')  80.6 us
    reduce_scatter x1, waiting for transfers between devices, shards(): lax.psum_scatter(dot(token_rows, grad_low, TN), 'dp', scatter_dimension=0...  76.9 us
    all_gather x1, waiting for transfers between devices, shards(): whole = lax.all_gather(weight_proj, 'dp', axis=0, tiled=True)  42.9 us
    dot_general x2, matrix products, dot(): return lax.dot_general(a, b, dims, preferred_element_type=f32)  12.4 us
    unnamed x13, local copies, waits for them, and re-layouts  9.66 us
  transfers between devices with their start and end apart: 3, of which 3 were waited for; matrix products, arithmetic and copies ran while one was open for 2% of the time, Pallas kernels for 0%

profile of v1, /device:TPU:0, one launch (start us, length us, event | category | flops | bytes accessed | tf_op | source)
XLA Modules:
  0.0 358.4 jit_solution(735966639574192829)
XLA Ops:
  7.2 0.0 all-gather.2.cloned.1.call-start
  7.2 0.7 all-gather.2.cloned.1.call-update
  7.9 0.0 reduce-scatter.2.cloned.1.call-start
  7.9 0.7 select_maximum_fusion.head_ref
  8.6 0.0 copy-start.1
  8.6 42.9 %all-gather.2.cloned.1.call-done = bf16[8192,320]{0,1:T(8,128)(2,1)} async-done(((bf16[512,320]{0,1:T(8,128)(2,1)}), bf16[8192,320]{0,1:T(8,128)(2,1)}) %all-gather.2.cloned.1.call-update) | async-done | bytes 5242896 | tf_op jit(solution)/shard_map/all_gather | solution.py:313
  51.6 6.1 %fusion.5.proj_ref = f32[256,384]{1,0:T(8,128)S(1)} fusion(bf16[1,256,8192]{2,1,0:T(8,128)(2,1)} %param.7, bf16[8192,320]{0,1:T(8,128)(2,1)} %all-gather.2.cloned.1.call-done), kind=kOutput, calls=%fused_computation.7 | convolution fusion | flops 1610612736 | bytes 9830400 | tf_op jit(solution)/shard_map/dot_general | solution.py:315
  57.7 0.0 copy-done.1
  57.7 0.0 copy-start.3
  57.7 114.5 %shard_map.102 = (bf16[256,8192]{1,0:T(8,128)(2,1)S(1)}, bf16[256,8192]{1,0:T(8,128)(2,1)}, bf16[256,384]{1,0:T(8,128)(2,1)S(1)}) custom-call(f32[64]{0:T(128)S(1)} %copy-done.1, f32[256,384]{1,0:T(8,128)S(1)} %fusion.5.proj_ref, f32[8,128]{1,0:T(8,128)S(1)} %select_maximum_fusion.head_ref, bf16[256,8192]{1,0:T(8,128)(2,1)} %bitcast.21, ...), custom_call_target="tpu_custom_call" | custom-call | tf_op jit(solution)/shard_map/pallas_call | solution.py:267
  172.2 0.0 copy-start
  172.2 2.0 copy-done
  174.2 0.0 copy-done.3
  174.2 5.5 %convolution_bitcast_fusion = f32[8192,320]{0,1:T(8,128)} fusion(bf16[1,256,8192]{2,1,0:T(8,128)(2,1)S(1)} %copy-done.3, bf16[256,384]{1,0:T(8,128)(2,1)S(1)} %get-tuple-element.9), kind=kOutput, calls=%fused_computation | convolution fusion | flops 1342177280 | bytes 14876672 | tf_op jit(solution)/shard_map/dot_general | solution.py:24
  179.8 0.0 reduce-scatter.2.cloned.1.call-update
  179.8 0.0 all-reduce.4.cloned.1.call-start
  179.8 76.9 %reduce-scatter.2.cloned.1.call-done = f32[512,320]{0,1:T(8,128)} async-done(((f32[8192,320]{0,1:T(8,128)}), f32[512,320]{0,1:T(8,128)}) %reduce-scatter.2.cloned.1.call-update) | async-done | bytes 655376 | tf_op jit(solution)/shard_map/reduce_scatter | solution.py:325
  256.7 0.0 all-reduce.4.cloned.1.call-update
  256.8 6.8 %fusion = bf16[1,256,8192]{2,1,0:T(8,128)(2,1)} fusion(bf16[8192,320]{0,1:T(8,128)(2,1)} %all-gather.2.cloned.1.call-done, bf16[256,384]{1,0:T(8,128)(2,1)S(1)} %get-tuple-element.9), kind=kOutput, calls=%fused_computation.2 | convolution fusion | flops 1344274432 | bytes 9633792 | tf_op jit(solution)/shard_map/dot_general | solution.py:24
  263.6 80.6 %all-reduce.4.cloned.1.call-done = f32[512,320]{0,1:T(8,128)} async-done(((f32[512,320]{0,1:T(8,128)}), f32[512,320]{0,1:T(8,128)}) %all-reduce.4.cloned.1.call-update) | async-done | bytes 655376 | tf_op jit(solution)/shard_map/psum | solution.py:328
  344.2 0.0 copy-start.2
  344.2 4.8 %copy.16 = bf16[1,256,8192]{2,1,0:T(8,128)(2,1)} copy(bf16[1,256,8192]{2,1,0:T(8,128)(2,1)} %bitcast.20) | data formatting | bytes 8388608
  349.0 0.0 copy-done.2
  349.0 0.0 copy-start.4
  349.0 2.0 copy.17
  351.0 0.0 copy-done.4
  351.0 0.8 copy.18
Async XLA Ops:
  7.2 44.4 %all-gather.2.cloned.1.call-start = ((), (), s32[]{:S(2)}) async-start(), calls=%async_computation.1 | async-start | bytes 5570560 | tf_op jit(solution)/shard_map/all_gather | solution.py:313
  7.9 248.8 %reduce-scatter.2.cloned.1.call-start = ((), (), s32[]{:S(2)}) async-start(), calls=%async_computation.2 | async-start | bytes 11141120 | tf_op jit(solution)/shard_map/reduce_scatter | solution.py:325
  8.6 49.1 %copy-start.1 = (f32[64]{0:T(128)S(1)}, f32[64]{0:T(128)}, u32[]{:S(2)}) copy-start(f32[64]{0:T(128)} %gain_ref.1) | copy-start | bytes 772
  57.7 116.5 %copy-start.3 = (bf16[1,256,8192]{2,1,0:T(8,128)(2,1)S(1)}, bf16[1,256,8192]{2,1,0:T(8,128)(2,1)}, u32[]{:S(2)}) copy-start(bf16[1,256,8192]{2,1,0:T(8,128)(2,1)} %param.7) | copy-start | bytes 12582916
  172.2 2.0 copy-start
  179.8 164.4 %all-reduce.4.cloned.1.call-start = ((), (), s32[]{:S(2)}) async-start(), calls=%async_computation.3 | async-start | bytes 1310720 | tf_op jit(solution)/shard_map/psum | solution.py:328
  344.2 4.8 %copy-start.2 = (bf16[256,8192]{1,0:T(8,128)(2,1)S(1)}, bf16[256,8192]{1,0:T(8,128)(2,1)}, u32[]{:S(2)}) copy-start(bf16[256,8192]{1,0:T(8,128)(2,1)} %get-tuple-element.8) | copy-start | bytes 12582916
  349.0 2.0 copy-start.4
Sparse Core Ops, SparseCore 0:
  9.7 41.8 all-gather.1
  179.9 76.8 reduce-scatter.1
  259.3 84.9 all-reduce.3

commit v2 on v1

--- a/solution.py
+++ b/solution.py
@@ -304,6 +304,248 @@
     )(gain, proj, head, x, dy)
 
 
+def weight_grad_kernel(
+    h_ref, g_ref, out_ref, g_t, sib_send, sib_recv, own, low,
+    slot_a0, slot_a1, slot_a2, sum_a0, sum_a1, sum_a2, low_a0, low_a1, low_a2,
+    slot_b0, slot_b1, slot_b2, sum_b0, sum_b1, sum_b2,
+    slot_c0, slot_c1, slot_c2, final, gathered,
+    sib_s, sib_r, st_s, st_r, ga_s, ga_r,
+):
+    dp = lax.axis_index("dp")
+    ctx = lax.axis_index("ctx")
+    x_lo, z, core = dp // 8, lax.rem(dp // 2, 4), lax.rem(dp, 2)
+    x_hi, y = ctx // 4, lax.rem(ctx, 4)
+    x = x_hi * 2 + x_lo
+    rows = out_ref.shape[0]
+    depth = out_ref.shape[1]
+    half = rows // 2
+    lanes = depth // 4
+
+    def device(x_lo=x_lo, z=z, core=core, x_hi=x_hi, y=y):
+        return {"dp": x_lo * 8 + z * 2 + core, "ctx": x_hi * 4 + y}
+
+    def ring(axis, d):
+        if axis == "z":
+            return device(z=lax.rem(z + d, 4)), (lax.rem(z + d, 4),)
+        if axis == "y":
+            return device(y=lax.rem(y + d, 4)), (lax.rem(y + d, 4),)
+        to = lax.rem(x + d, 4)
+        return device(x_lo=lax.rem(to, 2), x_hi=to // 2), (lax.rem(to, 2), to // 2)
+
+    barrier = pltpu.get_barrier_semaphore()
+    others = [(a, b) for a in range(2) for b in range(4) if a + b]
+    peers = [device(core=1 - core)]
+    peers += [ring("z", d)[0] for d in (1, 2, 3)]
+    peers += [ring("x", d)[0] for d in (1, 3)]
+    peers += [device(x_hi=lax.rem(x_hi + a, 2), y=lax.rem(y + b, 4)) for a, b in others]
+    for peer in peers:
+        pl.semaphore_signal(barrier, inc=1, device_id=peer, device_id_type=MESH)
+    g_t[...] = g_ref[...].astype(f32).T.astype(bf16)
+    pl.semaphore_wait(barrier, len(peers))
+
+    def product(s, side):
+        at = (s // 4) * 8 + lax.rem(s, 4) * 2 + side
+        block = h_ref[:, pl.ds(pl.multiple_of(at * depth, depth), depth)]
+        return dot(g_t[:rows, :], block)
+
+    def sib(s):
+        return pltpu.make_async_remote_copy(
+            src_ref=sib_send.at[s], dst_ref=sib_recv.at[s],
+            send_sem=sib_s.at[s], recv_sem=sib_r.at[s],
+            device_id=device(core=1 - core), device_id_type=MESH,
+        )
+
+    def for_sibling(s, carry):
+        p = product(s, 1 - core).astype(bf16)
+        for b in range(4):
+            for a in range(2):
+                sib_send[s, b, a] = p[a * half : (a + 1) * half, b * lanes : (b + 1) * lanes]
+        sib(s).start()
+        return carry
+
+    lax.fori_loop(0, 8, for_sibling, 0)
+
+    def for_self(s, carry):
+        p = product(s, core)
+        sib(s).wait_recv()
+        for b in range(4):
+            for a in range(2):
+                total = p[a * half : (a + 1) * half, b * lanes : (b + 1) * lanes]
+                total += sib_recv[s, b, a].astype(f32)
+                own[s // 4, lax.rem(s, 4), b, a] = total
+                low[s // 4, lax.rem(s, 4), b, a] = total.astype(bf16)
+        return carry
+
+    lax.fori_loop(0, 8, for_self, 0)
+
+    orders = (("z", "y", "x"), ("y", "x", "z"), ("x", "z", "y"))
+    slots = ((slot_a0, slot_b0, slot_c0), (slot_a1, slot_b1, slot_c1), (slot_a2, slot_b2, slot_c2))
+
+    def pick(left, axis, place):
+        at = []
+        for name in left:
+            if name == axis:
+                at.append(place[0])
+            elif axis == "x" and name == "x_lo":
+                at.append(place[0])
+            elif axis == "x" and name == "x_hi":
+                at.append(place[1])
+            else:
+                at.append(slice(None))
+        return tuple(at)
+
+    def rest(left, axis):
+        gone = ("x_lo", "x_hi") if axis == "x" else (axis,)
+        return tuple(name for name in left if name not in gone)
+
+    everything = ("x_lo", "z", "y", "x_hi")
+
+    def exchange(color, stage, source, left):
+        axis = orders[color][stage]
+        off, size = bands(half)[color]
+        window = (pl.ds(off, size),) if stage == 0 else ()
+        copies = []
+        for d in (1, 2, 3):
+            peer, place = ring(axis, d)
+            n = color * 9 + stage * 3 + d - 1
+            copies.append(
+                pltpu.make_async_remote_copy(
+                    src_ref=source.at[pick(left, axis, place) + window],
+                    dst_ref=slots[color][stage].at[d - 1],
+                    send_sem=st_s.at[n], recv_sem=st_r.at[n],
+                    device_id=peer, device_id_type=MESH,
+                )
+            )
+            copies[-1].start()
+        return copies
+
+    def my_place(axis):
+        return {"z": (z,), "y": (y,), "x": (x_lo, x_hi)}[axis]
+
+    pending = []
+    left = [everything] * 3
+    current = []
+    for color in range(3):
+        current.append(exchange(color, 0, low, everything))
+    sums = (sum_a0, sum_a1, sum_a2)
+    lows = (low_a0, low_a1, low_a2)
+    for color in range(3):
+        axis = orders[color][0]
+        off, size = bands(half)[color]
+        for copy in current[color]:
+            copy.wait_recv()
+        pending += current[color]
+        total = own[pick(everything, axis, my_place(axis)) + (pl.ds(off, size),)]
+        for d in range(3):
+            total += slots[color][0][d].astype(f32)
+        sums[color][...] = total
+        lows[color][...] = total.astype(bf16)
+        left[color] = rest(everything, axis)
+        current[color] = exchange(color, 1, lows[color], left[color])
+    finals = (sum_b0, sum_b1, sum_b2)
+    for color in range(3):
+        axis = orders[color][1]
+        for copy in current[color]:
+            copy.wait_recv()
+        pending += current[color]
+        total = sums[color][pick(left[color], axis, my_place(axis))]
+        for d in range(3):
+            total += slots[color][1][d].astype(f32)
+        finals[color][...] = total
+        left[color] = rest(left[color], axis)
+        current[color] = exchange(color, 2, finals[color], left[color])
+    gathers = []
+    for color in range(3):
+        axis = orders[color][2]
+        off, size = bands(half)[color]
+        for copy in current[color]:
+            copy.wait_recv()
+        pending += current[color]
+        total = finals[color][pick(left[color], axis, my_place(axis))]
+        for d in range(3):
+            total += slots[color][2][d]
+        final[pl.ds(off, size)] = total
+        for m, (a, b) in enumerate(others):
+            gathers.append(
+                pltpu.make_async_remote_copy(
+                    src_ref=final.at[pl.ds(off, size)],
+                    dst_ref=gathered.at[x_hi, y, pl.ds(off, size)],
+                    send_sem=ga_s.at[color * 7 + m], recv_sem=ga_r.at[color * 7 + m],
+                    device_id=device(x_hi=lax.rem(x_hi + a, 2), y=lax.rem(y + b, 4)),
+                    device_id_type=MESH,
+                )
+            )
+            gathers[-1].start()
+    for copy in gathers:
+        copy.wait_recv()
+    for a in range(2):
+        for b in range(4):
+            mine = (x_hi == a) & (y == b)
+            part = jnp.where(mine, final[...], gathered[a, b])
+            out_ref[a * half : (a + 1) * half, b * lanes : (b + 1) * lanes] = part
+    for copy in pending + gathers:
+        copy.wait_send()
+
+    def sent(s, carry):
+        sib(s).wait_send()
+        return carry
+
+    lax.fori_loop(0, 8, sent, 0)
+
+
+def bands(half):
+    third = half // 3 // 16 * 16
+    return ((0, third), (third, third), (2 * third, half - 2 * third))
+
+
+def weight_grad(token_rows, grad_low, cols, depth):
+    half, lanes = cols // 2, depth // 4
+    sizes = [size for _, size in bands(half)]
+    vm = pl.BlockSpec(memory_space=pltpu.VMEM)
+    dims = {"x_lo": 2, "z": 4, "y": 4, "x_hi": 2}
+    kept = (
+        (("x_lo", "y", "x_hi"), ("x_lo", "z", "x_hi"), ("z", "y")),
+        (("x_lo", "x_hi"), ("z",), ("y",)),
+        ((), (), ()),
+    )
+
+    def shape(stage, color):
+        return tuple(dims[name] for name in kept[stage][color]) + (sizes[color], lanes)
+
+    return pl.pallas_call(
+        weight_grad_kernel,
+        out_shape=jax.ShapeDtypeStruct((cols, depth), f32),
+        in_specs=[vm, vm],
+        out_specs=vm,
+        scratch_shapes=[
+            pltpu.VMEM((grad_low.shape[1], grad_low.shape[0]), bf16),
+            pltpu.VMEM((8, 4, 2, half, lanes), bf16),
+            pltpu.VMEM((8, 4, 2, half, lanes), bf16),
+            pltpu.VMEM((2, 4, 4, 2, half, lanes), f32),
+            pltpu.VMEM((2, 4, 4, 2, half, lanes), bf16),
+        ]
+        + [pltpu.VMEM((3,) + shape(0, c), bf16) for c in range(3)]
+        + [pltpu.VMEM(shape(0, c), f32) for c in range(3)]
+        + [pltpu.VMEM(shape(0, c), bf16) for c in range(3)]
+        + [pltpu.VMEM((3,) + shape(1, c), bf16) for c in range(3)]
+        + [pltpu.VMEM(shape(1, c), f32) for c in range(3)]
+        + [pltpu.VMEM((3,) + shape(2, c), f32) for c in range(3)]
+        + [
+            pltpu.VMEM((half, lanes), f32),
+            pltpu.VMEM((2, 4, half, lanes), f32),
+            pltpu.SemaphoreType.DMA((8,)),
+            pltpu.SemaphoreType.DMA((8,)),
+            pltpu.SemaphoreType.DMA((27,)),
+            pltpu.SemaphoreType.DMA((27,)),
+            pltpu.SemaphoreType.DMA((21,)),
+            pltpu.SemaphoreType.DMA((21,)),
+        ],
+        compiler_params=pltpu.CompilerParams(
+            collective_id=1, has_side_effects=True, vmem_limit_bytes=48 * 2**20
+        ),
+    )(token_rows, grad_low)
+
+
 def shards(pieces, hidden_rows, inner_rows, weight_proj, decay_log, step_bias, skip_gain, grad_output):
     token_rows = hidden_rows.reshape(-1, hidden_rows.shape[-1])
     value_rows = inner_rows.reshape(-1, inner_rows.shape[-1])
@@ -319,13 +561,9 @@
     )
     ssd_output = output.reshape(inner_rows.shape)
     grad_inner = grad_values.reshape(inner_rows.shape)
-    grad_low = grad_low[:, :cols]
-    grad_tokens = dot(grad_low, whole, NT)
+    grad_weight = weight_grad(token_rows, grad_low, cols, weight_proj.shape[0]).T
+    grad_tokens = dot(grad_low[:, :cols], whole, NT)
     grad_hidden = grad_tokens.astype(bf16).reshape(hidden_rows.shape)
-    grad_shard = lax.psum_scatter(
-        dot(token_rows, grad_low, TN), "dp", scatter_dimension=0, tiled=True
-    )
-    grad_weight = lax.psum(grad_shard, "ctx")
     return (ssd_output, grad_inner, grad_hidden, grad_weight)
 
 

time: 359 us -> 235 us (0.65)
  waiting for transfers between devices: 201 us -> 43.7 us
  Pallas kernels: 114 us -> 157 us
  matrix products: 18.5 us -> 12.9 us
    psum x1 -> x0, waiting for transfers between devices: 80.6 us -> none  [shards(): grad_weight = lax.psum(grad_shard, 'ctx')]
    reduce_scatter x1 -> x0, waiting for transfers between devices: 76.9 us -> none  [shards(): lax.psum_scatter(dot(token_rows, grad_low, TN), 'dp', scatter_dimension=0...]
    pallas_call x0 -> x1, Pallas kernels: none -> 42.3 us  [weight_grad(): pl.pallas_call(weight_grad_kernel, out_shape=jax.ShapeDtypeStruct((cols,...]
    dot_general x2 -> x1, matrix products: 12.4 us -> 6.84 us  [dot(): return lax.dot_general(a, b, dims, preferred_element_type=f32)]
    unnamed x13 -> x9, local copies, waits for them, and re-layouts: 9.66 us -> 6.56 us
  transfers between devices with their start and end apart: 3 -> 1, of which waited for: 3 -> 1; matrix products, arithmetic and copies ran while one was open for 2% -> 0% of each run, Pallas kernels for 0% -> 0%
where the time goes in v2:
time: 235 us
  Pallas kernels  157 us (67%)
  waiting for transfers between devices  43.7 us (19%)
  between operations  14.1 us (6%)
  matrix products  12.9 us (5%)
  local copies, waits for them, and re-layouts  6.56 us (3%)
    pallas_call x1, Pallas kernels, scan_pass(): pl.pallas_call(partial(scan_kernel, pieces, heads), out_shape=(jax.ShapeD...  114 us
    all_gather x1, waiting for transfers between devices, shards(): whole = lax.all_gather(weight_proj, 'dp', axis=0, tiled=True)  43 us
    pallas_call x1, Pallas kernels, weight_grad(): pl.pallas_call(weight_grad_kernel, out_shape=jax.ShapeDtypeStruct((cols,...  42.3 us
    dot_general x1, matrix products, dot(): return lax.dot_general(a, b, dims, preferred_element_type=f32)  6.84 us
    unnamed x9, local copies, waits for them, and re-layouts  6.56 us
    dot_general x1, matrix products, shards(): projected = jnp.dot(token_rows, padded, preferred_element_type=f32)  6.1 us
  transfers between devices with their start and end apart: 1, of which 1 were waited for; matrix products, arithmetic and copies ran while one was open for 0% of the time, Pallas kernels for 0%

profile of v2, /device:TPU:0, one launch (start us, length us, event | category | flops | bytes accessed | tf_op | source)
XLA Modules:
  0.0 234.7 jit_solution(12028575293061058688)
XLA Ops:
  7.2 0.0 all-gather.2.cloned.1.call-start
  7.2 0.7 all-gather.2.cloned.1.call-update
  7.9 0.7 select_maximum_fusion.head_ref
  8.6 0.0 copy-start.1
  8.6 43.0 %all-gather.2.cloned.1.call-done = bf16[8192,320]{0,1:T(8,128)(2,1)} async-done(((bf16[512,320]{0,1:T(8,128)(2,1)}), bf16[8192,320]{0,1:T(8,128)(2,1)}) %all-gather.2.cloned.1.call-update) | async-done | bytes 5242896 | tf_op jit(solution)/shard_map/all_gather | solution.py:555
  51.6 6.1 %fusion.3.proj_ref = f32[256,384]{1,0:T(8,128)S(1)} fusion(bf16[8192,320]{0,1:T(8,128)(2,1)} %all-gather.2.cloned.1.call-done, bf16[1,256,8192]{2,1,0:T(8,128)(2,1)} %param.7), kind=kOutput, calls=%fused_computation.4 | convolution fusion | flops 1610612736 | bytes 9830400 | tf_op jit(solution)/shard_map/dot_general | solution.py:557
  57.7 0.0 copy-done.1
  57.7 0.0 copy-start
  57.7 114.4 %shard_map.102 = (bf16[256,8192]{1,0:T(8,128)(2,1)S(1)}, bf16[256,8192]{1,0:T(8,128)(2,1)}, bf16[256,384]{1,0:T(8,128)(2,1)S(1)}) custom-call(f32[64]{0:T(128)S(1)} %copy-done.1, f32[256,384]{1,0:T(8,128)S(1)} %fusion.3.proj_ref, f32[8,128]{1,0:T(8,128)S(1)} %select_maximum_fusion.head_ref, bf16[256,8192]{1,0:T(8,128)(2,1)} %bitcast.18, ...), custom_call_target="tpu_custom_call" | custom-call | tf_op jit(solution)/shard_map/pallas_call | solution.py:267
  172.1 0.0 copy-done
  172.1 42.3 %shard_map.103 = f32[320,512]{1,0:T(8,128)S(1)} custom-call(bf16[256,8192]{1,0:T(8,128)(2,1)S(1)} %bitcast.15, bf16[256,384]{1,0:T(8,128)(2,1)S(1)} %get-tuple-element.9.g_ref), custom_call_target="tpu_custom_call" | custom-call | tf_op jit(solution)/shard_map/pallas_call | solution.py:515
  214.5 6.8 %fusion = bf16[1,256,8192]{2,1,0:T(8,128)(2,1)} fusion(bf16[8192,320]{0,1:T(8,128)(2,1)} %all-gather.2.cloned.1.call-done, bf16[256,384]{1,0:T(8,128)(2,1)S(1)} %get-tuple-element.9.g_ref), kind=kOutput, calls=%fused_computation.1 | convolution fusion | flops 1344274432 | bytes 9633792 | tf_op jit(solution)/shard_map/dot_general | solution.py:24
  221.3 0.0 copy-start.2
  221.3 2.1 copy.16
  223.4 1.6 copy-done.2
  225.0 2.0 copy.17
  227.0 0.8 copy.18
Async XLA Ops:
  7.2 44.4 %all-gather.2.cloned.1.call-start = ((), (), s32[]{:S(2)}) async-start(), calls=%async_computation | async-start | bytes 5570560 | tf_op jit(solution)/shard_map/all_gather | solution.py:555
  8.6 49.1 %copy-start.1 = (f32[64]{0:T(128)S(1)}, f32[64]{0:T(128)}, u32[]{:S(2)}) copy-start(f32[64]{0:T(128)} %gain_ref.1) | copy-start | bytes 772
  57.7 114.4 %copy-start = (bf16[1,256,8192]{2,1,0:T(8,128)(2,1)S(1)}, bf16[1,256,8192]{2,1,0:T(8,128)(2,1)}, u32[]{:S(2)}) copy-start(bf16[1,256,8192]{2,1,0:T(8,128)(2,1)} %param.7) | copy-start | bytes 12582916
  221.3 3.7 %copy-start.2 = (bf16[256,8192]{1,0:T(8,128)(2,1)S(1)}, bf16[256,8192]{1,0:T(8,128)(2,1)}, u32[]{:S(2)}) copy-start(bf16[256,8192]{1,0:T(8,128)(2,1)} %get-tuple-element.8) | copy-start | bytes 12582916
Sparse Core Ops, SparseCore 0:
  9.7 41.8 all-gather.1

commit v3 on v2

--- a/solution.py
+++ b/solution.py
@@ -10,7 +10,7 @@
 PS = 128
 NS = 128
 CHUNK = 2
-LAG = 2
+LAG = 4
 MESH = pl.DeviceIdType.MESH
 highest = lax.Precision.HIGHEST
 f32 = jnp.float32
@@ -546,15 +546,187 @@
     )(token_rows, grad_low)
 
 
+def project_kernel(
+    w_ref, h_ref, proj_ref, all_ref, st_s, st_r, sib_s, sib_r
+):
+    dp = lax.axis_index("dp")
+    ctx = lax.axis_index("ctx")
+    x_lo, z, core = dp // 8, lax.rem(dp // 2, 4), lax.rem(dp, 2)
+    x_hi, y = ctx // 4, lax.rem(ctx, 4)
+    x = x_hi * 2 + x_lo
+    cols, depth = w_ref.shape
+    half, lanes = cols // 2, depth // 4
+
+    def device(x_lo=x_lo, z=z, core=core, x_hi=x_hi, y=y):
+        return {"dp": x_lo * 8 + z * 2 + core, "ctx": x_hi * 4 + y}
+
+    def ring(axis, d):
+        if axis == "z":
+            return device(z=lax.rem(z + d, 4))
+        if axis == "y":
+            return device(y=lax.rem(y + d, 4))
+        to = lax.rem(x + d, 4)
+        return device(x_lo=lax.rem(to, 2), x_hi=to // 2)
+
+    barrier = pltpu.get_barrier_semaphore()
+    peers = [device(core=1 - core)]
+    peers += [ring(axis, d) for axis in "xyz" for d in (1, 2, 3)]
+    for peer in peers:
+        pl.semaphore_signal(barrier, inc=1, device_id=peer, device_id_type=MESH)
+    for a in range(2):
+        for b in range(4):
+            @pl.when((x_hi == a) & (y == b))
+            def _():
+                all_ref[core, x_lo, z, b, a] = w_ref[
+                    a * half : (a + 1) * half, b * lanes : (b + 1) * lanes
+                ]
+    proj_ref[...] = jnp.zeros_like(proj_ref)
+    pl.semaphore_wait(barrier, len(peers))
+
+    whole = slice(None)
+    orders = ("xyz", "zxy", "yzx")
+
+    def region(side, color, have, x_lo=x_lo, z=z, x_hi=x_hi, y=y):
+        off, size = bands(half)[color]
+        return all_ref.at[
+            side,
+            whole if "x" in have else x_lo,
+            whole if "z" in have else z,
+            whole if "y" in have else y,
+            whole if "x" in have else x_hi,
+            pl.ds(off, size),
+        ]
+
+    def exchange(color, stage):
+        axis = orders[color][stage]
+        copies = []
+        for d in (1, 2, 3):
+            n = color * 9 + stage * 3 + d - 1
+            part = region(core, color, orders[color][:stage])
+            copies.append(
+                pltpu.make_async_remote_copy(
+                    src_ref=part, dst_ref=part, send_sem=st_s.at[n], recv_sem=st_r.at[n],
+                    device_id=ring(axis, d), device_id_type=MESH,
+                )
+            )
+            copies[-1].start()
+        return copies
+
+    def origin(axis, d):
+        if axis == "z":
+            return {"z": lax.rem(z + 4 - d, 4)}
+        if axis == "y":
+            return {"y": lax.rem(y + 4 - d, 4)}
+        at = lax.rem(x + 4 - d, 4)
+        return {"x_lo": lax.rem(at, 2), "x_hi": at // 2}
+
+    def to_sibling(color, d):
+        place = origin(orders[color][2], d) if d else {}
+        part = region(core, color, orders[color][:2], **place)
+        copy = pltpu.make_async_remote_copy(
+            src_ref=part, dst_ref=part,
+            send_sem=sib_s.at[color * 4 + d], recv_sem=sib_r.at[color * 4 + d],
+            device_id=device(core=1 - core), device_id_type=MESH,
+        )
+        copy.start()
+        return copy
+
+    pending, current, shared = [], [], []
+    for color in range(3):
+        current.append(exchange(color, 0))
+    for stage in (1, 2):
+        for color in range(3):
+            for copy in current[color]:
+                copy.wait_recv()
+            pending += current[color]
+            current[color] = exchange(color, stage)
+            if stage == 2:
+                shared.append(to_sibling(color, 0))
+    for d in (1, 3, 2):
+        for color in range(3):
+            current[color][d - 1].wait_recv()
+            shared.append(to_sibling(color, d))
+    for color in range(3):
+        pending += current[color]
+
+    def add(s, side):
+        at = (s // 4) * 8 + lax.rem(s, 4) * 2 + side
+        block = h_ref[:, pl.ds(pl.multiple_of(at * depth, depth), depth)]
+        weights = jnp.concatenate(
+            [all_ref[side, s // 4, lax.rem(s, 4), b].reshape(cols, lanes) for b in range(4)],
+            axis=1,
+        )
+        proj_ref[:, :cols] += dot(block, weights, NT)
+
+    def mine(s, carry):
+        add(s, core)
+        return carry
+
+    def other(s, carry):
+        add(s, 1 - core)
+        return carry
+
+    lax.fori_loop(0, 8, mine, 0)
+    for copy in shared:
+        copy.wait_recv()
+    lax.fori_loop(0, 8, other, 0)
+    for copy in pending + shared:
+        copy.wait_send()
+
+
+def project(weight_t, token_rows):
+    cols, depth = weight_t.shape
+    vm = pl.BlockSpec(memory_space=pltpu.VMEM)
+    return pl.pallas_call(
+        project_kernel,
+        out_shape=(
+            jax.ShapeDtypeStruct((token_rows.shape[0], 3 * NS), f32),
+            jax.ShapeDtypeStruct((2, 2, 4, 4, 2, cols // 2, depth // 4), bf16),
+        ),
+        in_specs=[vm, vm],
+        out_specs=(vm, vm),
+        scratch_shapes=[
+            pltpu.SemaphoreType.DMA((27,)),
+            pltpu.SemaphoreType.DMA((27,)),
+            pltpu.SemaphoreType.DMA((12,)),
+            pltpu.SemaphoreType.DMA((12,)),
+        ],
+        compiler_params=pltpu.CompilerParams(
+            collective_id=2, has_side_effects=True, vmem_limit_bytes=40 * 2**20
+        ),
+    )(weight_t, token_rows)
+
+
+def hidden_kernel(g_ref, w_ref, out_ref):
+    cols = w_ref.shape[2] * w_ref.shape[3]
+    weights = jnp.concatenate([w_ref[0, b].reshape(cols, -1) for b in range(4)], axis=1)
+    out_ref[...] = dot(g_ref[:, :cols], weights).astype(bf16)
+
+
+def hidden_grad(grad_low, weights):
+    tokens = grad_low.shape[0]
+    half, lanes = weights.shape[-2:]
+    depth = 4 * lanes
+    flat = weights.reshape(2 * 8, 4, 2, half, lanes)
+    return pl.pallas_call(
+        hidden_kernel,
+        grid=(16,),
+        out_shape=jax.ShapeDtypeStruct((tokens, 16 * depth), bf16),
+        in_specs=[
+            pl.BlockSpec(grad_low.shape, lambda i: (0, 0)),
+            pl.BlockSpec((1, 4, 2, half, lanes), lambda i: (i, 0, 0, 0, 0)),
+        ],
+        out_specs=pl.BlockSpec((tokens, depth), lambda i: (0, (i % 8) * 2 + i // 8)),
+    )(grad_low, flat)
+
+
 def shards(pieces, hidden_rows, inner_rows, weight_proj, decay_log, step_bias, skip_gain, grad_output):
     token_rows = hidden_rows.reshape(-1, hidden_rows.shape[-1])
     value_rows = inner_rows.reshape(-1, inner_rows.shape[-1])
     cotangent = grad_output.reshape(value_rows.shape)
     cols = weight_proj.shape[1]
     heads = decay_log.shape[0]
-    whole = lax.all_gather(weight_proj, "dp", axis=0, tiled=True)
-    padded = jnp.pad(whole, ((0, 0), (0, 3 * NS - cols)))
-    projected = jnp.dot(token_rows, padded, preferred_element_type=f32)
+    projected, weights = project(weight_proj.T, token_rows)
     head = jnp.pad(jnp.stack([step_bias, decay_log]), ((0, 6), (0, NS - heads)))
     output, grad_values, grad_low = scan_pass(
         pieces, skip_gain, projected, head, value_rows, cotangent
@@ -562,8 +734,7 @@
     ssd_output = output.reshape(inner_rows.shape)
     grad_inner = grad_values.reshape(inner_rows.shape)
     grad_weight = weight_grad(token_rows, grad_low, cols, weight_proj.shape[0]).T
-    grad_tokens = dot(grad_low[:, :cols], whole, NT)
-    grad_hidden = grad_tokens.astype(bf16).reshape(hidden_rows.shape)
+    grad_hidden = hidden_grad(grad_low, weights).reshape(hidden_rows.shape)
     return (ssd_output, grad_inner, grad_hidden, grad_weight)
 
 

time: 235 us -> 196 us (0.83)
  waiting for transfers between devices: 43.7 us -> 0 us
  Pallas kernels: 157 us -> 177 us
  between operations: 14.1 us -> 0.71 us
  matrix products: 12.9 us -> 0 us
  local copies, waits for them, and re-layouts: 6.56 us -> 16.9 us
    pallas_call x0 -> x2, Pallas kernels: none -> 45.2 us  [the longest x1 32.7 us: project(): pl.pallas_call(project_kernel, out_shape=(jax.ShapeDtypeStruct((token_row...]
    all_gather x1 -> x0, waiting for transfers between devices: 43 us -> none  [shards(): whole = lax.all_gather(weight_proj, 'dp', axis=0, tiled=True)]
    pallas_call x1, Pallas kernels: 114 us -> 92.3 us  [scan_pass(): pl.pallas_call(partial(scan_kernel, pieces, heads), out_shape=(jax.ShapeD...]
    dot_general x2 -> x0, matrix products: 12.9 us -> none  [the longest x1 6.84 us: dot(): return lax.dot_general(a, b, dims, preferred_element_type=f32)]
    unnamed x9 -> x23, local copies, waits for them, and re-layouts: 6.56 us -> 16.9 us
    pallas_call x1, Pallas kernels: 42.3 us -> 39.7 us  [weight_grad(): pl.pallas_call(weight_grad_kernel, out_shape=jax.ShapeDtypeStruct((cols,...]
  transfers between devices with their start and end apart: 1 -> 0, of which waited for: 1 -> 0; matrix products, arithmetic and copies ran while one was open for 0% -> 0% of each run, Pallas kernels for 0% -> 0%
where the time goes in v3:
time: 196 us; the launch traced here: 195 us
  Pallas kernels  177 us (90%)
  local copies, waits for them, and re-layouts  16.9 us (9%)
    pallas_call x1, Pallas kernels, scan_pass(): pl.pallas_call(partial(scan_kernel, pieces, heads), out_shape=(jax.ShapeD...  92.3 us
    pallas_call x1, Pallas kernels, weight_grad(): pl.pallas_call(weight_grad_kernel, out_shape=jax.ShapeDtypeStruct((cols,...  39.7 us
    pallas_call x1, Pallas kernels, project(): pl.pallas_call(project_kernel, out_shape=(jax.ShapeDtypeStruct((token_row...  32.7 us
    unnamed x23, local copies, waits for them, and re-layouts  16.9 us
    pallas_call x1, Pallas kernels, hidden_grad(): pl.pallas_call(hidden_kernel, grid=(16,), out_shape=jax.ShapeDtypeStruct(...  12.5 us

profile of v3, /device:TPU:0, one launch (start us, length us, event | category | flops | bytes accessed | tf_op | source)
XLA Modules:
  0.0 195.4 jit_solution(7526071658085487887)
XLA Ops:
  0.6 0.0 copy-start.8
  0.6 0.7 select_maximum_fusion.head_ref
  1.3 0.0 copy-start
  1.3 2.2 %copy-done = bf16[1,256,8192]{2,1,0:T(8,128)(2,1)S(1)} copy-done((bf16[1,256,8192]{2,1,0:T(8,128)(2,1)S(1)}, bf16[1,256,8192]{2,1,0:T(8,128)(2,1)}, u32[]{:S(2)}) %copy-start) | copy-done | bytes 4194328
  3.5 0.0 copy-start.7
  3.5 1.0 copy-done.7
  4.5 32.7 %shard_map.102 = (f32[256,384]{1,0:T(8,128)S(1)}, bf16[2,2,4,4,2,160,128]{6,5,4,3,2,1,0:T(8,128)(2,1)S(1)}) custom-call(bf16[320,512]{1,0:T(8,128)(2,1)S(1)} %bitcast.16, bf16[256,8192]{1,0:T(8,128)(2,1)S(1)} %bitcast.11), custom_call_target="tpu_custom_call" | custom-call | tf_op jit(solution)/shard_map/pallas_call | solution.py:680
  37.2 0.0 copy-start.2
  37.2 2.3 %copy-done.2 = bf16[2,2,4,4,2,160,128]{6,5,4,3,2,1,0:T(8,128)(2,1)} copy-done((bf16[2,2,4,4,2,160,128]{6,5,4,3,2,1,0:T(8,128)(2,1)}, bf16[2,2,4,4,2,160,128]{6,5,4,3,2,1,0:T(8,128)(2,1)S(1)}, u32[]{:S(2)}) %copy-start.2) | copy-done | bytes 5242904
  39.5 0.0 copy-done.8
  39.5 92.3 %shard_map.103 = (bf16[256,8192]{1,0:T(8,128)(2,1)S(1)}, bf16[256,8192]{1,0:T(8,128)(2,1)}, bf16[256,384]{1,0:T(8,128)(2,1)S(1)}) custom-call(f32[64]{0:T(128)S(1)} %copy-done.8, f32[256,384]{1,0:T(8,128)S(1)} %get-tuple-element.9.proj_ref, f32[8,128]{1,0:T(8,128)S(1)} %select_maximum_fusion.head_ref, bf16[256,8192]{1,0:T(8,128)(2,1)} %bitcast.18, ...), custom_call_target="tpu_custom_call" | custom-call | tf_op jit(solution)/shard_map/pallas_call | solution.py:267
  131.8 0.0 copy-start.3
  131.8 2.0 %copy-done.3 = bf16[256,8192]{1,0:T(8,128)(2,1)} copy-done((bf16[256,8192]{1,0:T(8,128)(2,1)}, bf16[256,8192]{1,0:T(8,128)(2,1)S(1)}, u32[]{:S(2)}) %copy-start.3) | copy-done | bytes 4194328
  133.8 0.0 copy-start.5
  133.8 0.7 copy-done.5
  134.5 0.0 copy-start.6
  134.5 12.5 %shard_map.104 = bf16[256,8192]{1,0:T(8,128)(2,1)} custom-call(bf16[256,384]{1,0:T(8,128)(2,1)} %copy-done.5, bf16[16,4,2,160,128]{4,3,2,1,0:T(8,128)(2,1)} %bitcast.13), custom_call_target="tpu_custom_call" | custom-call | tf_op jit(solution)/shard_map/pallas_call | solution.py:711
  147.0 0.0 copy-done.6
  147.0 0.0 copy-start.1
  147.0 2.2 %copy-done.1 = bf16[1,256,8192]{2,1,0:T(8,128)(2,1)S(1)} copy-done((bf16[1,256,8192]{2,1,0:T(8,128)(2,1)S(1)}, bf16[1,256,8192]{2,1,0:T(8,128)(2,1)}, u32[]{:S(2)}) %copy-start.1) | copy-done | bytes 4194328
  149.2 0.0 copy-start.4
  149.2 39.7 %shard_map.105 = f32[320,512]{1,0:T(8,128)S(1)} custom-call(bf16[256,8192]{1,0:T(8,128)(2,1)S(1)} %bitcast.12, bf16[256,384]{1,0:T(8,128)(2,1)S(1)} %copy-done.6), custom_call_target="tpu_custom_call" | custom-call | tf_op jit(solution)/shard_map/pallas_call | solution.py:515
  188.9 0.0 copy-done.4
  188.9 0.0 copy-start.9
  188.9 2.1 %copy.14 = bf16[1,256,8192]{2,1,0:T(8,128)(2,1)} copy(bf16[1,256,8192]{2,1,0:T(8,128)(2,1)S(1)} %bitcast.14) | data formatting | bytes 8388608
  191.0 1.6 copy-done.9
  192.6 2.0 %copy.15 = bf16[1,256,8192]{2,1,0:T(8,128)(2,1)} copy(bf16[1,256,8192]{2,1,0:T(8,128)(2,1)S(1)} %bitcast.20) | data formatting | bytes 8388608
  194.6 0.8 copy.16
Async XLA Ops:
  0.6 38.9 %copy-start.8 = (f32[64]{0:T(128)S(1)}, f32[64]{0:T(128)}, u32[]{:S(2)}) copy-start(f32[64]{0:T(128)} %gain_ref.1) | copy-start | bytes 772
  1.3 2.2 %copy-start = (bf16[1,256,8192]{2,1,0:T(8,128)(2,1)S(1)}, bf16[1,256,8192]{2,1,0:T(8,128)(2,1)}, u32[]{:S(2)}) copy-start(bf16[1,256,8192]{2,1,0:T(8,128)(2,1)} %param.7) | copy-start | bytes 12582916
  3.5 1.0 copy-start.7
  37.2 2.3 %copy-start.2 = (bf16[2,2,4,4,2,160,128]{6,5,4,3,2,1,0:T(8,128)(2,1)}, bf16[2,2,4,4,2,160,128]{6,5,4,3,2,1,0:T(8,128)(2,1)S(1)}, u32[]{:S(2)}) copy-start(bf16[2,2,4,4,2,160,128]{6,5,4,3,2,1,0:T(8,128)(2,1)S(1)} %get-tuple-element.13) | copy-start | bytes 15728644
  131.8 2.0 %copy-start.3 = (bf16[256,8192]{1,0:T(8,128)(2,1)}, bf16[256,8192]{1,0:T(8,128)(2,1)S(1)}, u32[]{:S(2)}) copy-start(bf16[256,8192]{1,0:T(8,128)(2,1)S(1)} %get-tuple-element.10) | copy-start | bytes 12582916
  133.8 0.7 copy-start.5
  134.5 12.5 %copy-start.6 = (bf16[256,384]{1,0:T(8,128)(2,1)S(1)}, bf16[256,384]{1,0:T(8,128)(2,1)}, u32[]{:S(2)}) copy-start(bf16[256,384]{1,0:T(8,128)(2,1)} %copy-done.5) | copy-start | bytes 589828
  147.0 2.2 %copy-start.1 = (bf16[1,256,8192]{2,1,0:T(8,128)(2,1)S(1)}, bf16[1,256,8192]{2,1,0:T(8,128)(2,1)}, u32[]{:S(2)}) copy-start(bf16[1,256,8192]{2,1,0:T(8,128)(2,1)} %param.7) | copy-start | bytes 12582916
  149.2 39.7 %copy-start.4 = (bf16[256,8192]{1,0:T(8,128)(2,1)S(1)}, bf16[256,8192]{1,0:T(8,128)(2,1)}, u32[]{:S(2)}) copy-start(bf16[256,8192]{1,0:T(8,128)(2,1)} %copy-done.3) | copy-start | bytes 12582916
  188.9 3.7 %copy-start.9 = (bf16[256,8192]{1,0:T(8,128)(2,1)S(1)}, bf16[256,8192]{1,0:T(8,128)(2,1)}, u32[]{:S(2)}) copy-start(bf16[256,8192]{1,0:T(8,128)(2,1)} %get-tuple-element.11) | copy-start | bytes 12582916

commit v4 on v1

v4 whole, which is shorter than its diff:
```python
from functools import partial

import jax
import jax.numpy as jnp
from jax import lax
from jax.experimental import pallas as pl
from jax.experimental.pallas import tpu as pltpu
from jax.sharding import PartitionSpec as P

PS = 128
NS = 128
CHUNK = 2
LAG = 2
LAG_FAR = 4
MESH = pl.DeviceIdType.MESH
highest = lax.Precision.HIGHEST
f32 = jnp.float32
bf16 = jnp.bfloat16
NN = (((1,), (0,)), ((), ()))
NT = (((1,), (1,)), ((), ()))
TN = (((0,), (0,)), ((), ()))


def dot(a, b, dims=NN):
    return lax.dot_general(a, b, dims, preferred_element_type=f32)


def dot_high(a, b, dims=NN):
    return lax.dot_general(a, b, dims, preferred_element_type=f32, precision=highest)


def split(a):
    high = a.astype(bf16)
    return high, (a - high.astype(f32)).astype(bf16)

BANDS = 3
ORDER_SUM = ("zyx", "yxz", "xzy")
ORDER_GATHER = ("xyz", "zxy", "yzx")


def bands(half):
    third = half // 3 // 16 * 16
    return ((0, third), (third, third), (2 * third, half - 2 * third))


def remote(src, dst, send, recv, device):
    return pltpu.make_async_remote_copy(
        src_ref=src, dst_ref=dst, send_sem=send, recv_sem=recv,
        device_id=device, device_id_type=MESH,
    )


class Place:
    def __init__(self):
        dp, ctx = lax.axis_index("dp"), lax.axis_index("ctx")
        self.x_lo, self.z, self.core = dp // 8, lax.rem(dp // 2, 4), lax.rem(dp, 2)
        self.x_hi, self.y = ctx // 4, lax.rem(ctx, 4)
        self.x = self.x_hi * 2 + self.x_lo
        self.ctx = ctx

    def device(self, **other):
        at = {name: getattr(self, name) for name in ("x_lo", "z", "core", "x_hi", "y")}
        at.update(other)
        return {
            "dp": at["x_lo"] * 8 + at["z"] * 2 + at["core"],
            "ctx": at["x_hi"] * 4 + at["y"],
        }

    def along(self, axis, d):
        to = lax.rem(getattr(self, axis) + d, 4)
        return {"x_lo": lax.rem(to, 2), "x_hi": to // 2} if axis == "x" else {axis: to}

    def ring(self, axis, d):
        return self.device(**self.along(axis, d))

    def sibling(self):
        return self.device(core=1 - self.core)

    def piece(self, a, b):
        return self.device(x_hi=lax.rem(self.x_hi + a, 2), y=lax.rem(self.y + b, 4))

    def columns(self, s, side, depth):
        at = (s // 4) * 8 + lax.rem(s, 4) * 2 + side
        return pl.ds(pl.multiple_of(at * depth, depth), depth)


OTHERS = [(a, b) for a in range(2) for b in range(4) if a + b]


def loop(count, body):
    def step(i, carry):
        body(i)
        return carry

    lax.fori_loop(0, count, step, 0)


def gather_weights(me, w_ref, all_ref, send, recv):
    cols, depth = w_ref.shape
    half = cols // 2
    whole = slice(None)

    def region(color, have):
        off, size = bands(half)[color]
        return all_ref.at[
            whole if "x" in have else me.x_lo,
            whole if "z" in have else me.z,
            whole if "y" in have else me.y,
            whole if "x" in have else me.x_hi,
            pl.ds(off, size),
        ]

    def exchange(color, stage):
        axis = ORDER_GATHER[color][stage]
        part = region(color, ORDER_GATHER[color][:stage])
        copies = []
        for d in (1, 3, 2):
            n = color * 9 + stage * 3 + d - 1
            copies.append(remote(part, part, send.at[n], recv.at[n], me.ring(axis, d)))
            copies[-1].start()
        return copies

    pending = []
    current = [exchange(color, 0) for color in range(BANDS)]
    for stage in (1, 2, 3):
        for color in range(BANDS):
            for copy in current[color]:
                copy.wait_recv()
            pending += current[color]
            if stage < 3:
                current[color] = exchange(color, stage)
    return pending


def sum_start(me, low, slots, send, recv):
    return [sum_exchange(me, color, 0, low, "xzy", slots, send, recv) for color in range(BANDS)]


def pick(left, axis, place):
    at = []
    for name in ("x_lo", "z", "y", "x_hi"):
        if name[0] in left:
            at.append(place[name] if name[0] == axis else slice(None))
    return tuple(at)


def sum_exchange(me, color, stage, source, left, slots, send, recv):
    axis = ORDER_SUM[color][stage]
    off, size = bands(slots[0][2].shape[1] + slots[1][2].shape[1] + slots[2][2].shape[1])[color]
    window = (pl.ds(off, size),) if stage == 0 else ()
    copies = []
    for d in (1, 3, 2):
        n = color * 9 + stage * 3 + d - 1
        part = source.at[pick(left, axis, me.along(axis, d)) + window]
        copies.append(
            remote(part, slots[color][stage].at[d - 1], send.at[n], recv.at[n], me.ring(axis, d))
        )
        copies[-1].start()
    return copies


def sum_finish(me, current, own, slots, sums, lows, finals, final, gathered, out_ref, send, recv, ga_s, ga_r):
    half = final.shape[0]
    lanes = final.shape[1]
    pending = []

    def arrived(color, stage, source, left, window=()):
        axis = ORDER_SUM[color][stage]
        pending.extend(current[color])
        for copy in current[color]:
            copy.wait_recv()
        total = source[pick(left, axis, me.along(axis, 0)) + window]
        for d in range(3):
            total += slots[color][stage][d].astype(f32)
        return total

    for color in range(BANDS):
        off, size = bands(half)[color]
        total = arrived(color, 0, own, "xzy", (pl.ds(off, size),))
        sums[color][...] = total
        lows[color][...] = total.astype(bf16)
        left = ORDER_SUM[color][1:]
        current[color] = sum_exchange(me, color, 1, lows[color], left, slots, send, recv)
    for color in range(BANDS):
        finals[color][...] = arrived(color, 1, sums[color], ORDER_SUM[color][1:])
        left = ORDER_SUM[color][2:]
        current[color] = sum_exchange(me, color, 2, finals[color], left, slots, send, recv)
    gathers = []
    for color in range(BANDS):
        off, size = bands(half)[color]
        final[pl.ds(off, size)] = arrived(color, 2, finals[color], ORDER_SUM[color][2:])
        for m, (a, b) in enumerate(OTHERS):
            n = color * 7 + m
            gathers.append(
                remote(
                    final.at[pl.ds(off, size)], gathered.at[me.x_hi, me.y, pl.ds(off, size)],
                    ga_s.at[n], ga_r.at[n], me.piece(a, b),
                )
            )
            gathers[-1].start()
    for copy in gathers:
        copy.wait_recv()
    for a in range(2):
        for b in range(4):
            mine = (me.x_hi == a) & (me.y == b)
            part = jnp.where(mine, final[...], gathered[a, b])
            out_ref[a * half : (a + 1) * half, b * lanes : (b + 1) * lanes] = part
    return pending + gathers


def layer_kernel(
    heads, gain_ref, head_ref, w_ref, h_ref, x_hbm, dy_hbm,
    y_hbm, dx_hbm, hid_hbm, gw_ref,
    h_all, w_all, x_ref, dy_ref, part, proj_in, proj_ref,
    run, run_t, step_t, step_c, key_t, query_t, key_hl, query_hl, scores,
    acc_diff, acc_cross, acc_const, dq, dk, dscores,
    state_in, state_out, grad_in, grad_out,
    g_all, gt_all, own, low,
    slot_a0, slot_a1, slot_a2, sum_a0, sum_a1, sum_a2, low_a0, low_a1, low_a2,
    slot_b0, slot_b1, slot_b2, sum_b0, sum_b1, sum_b2,
    slot_c0, slot_c1, slot_c2, final, gathered, hid,
    load_h, load_xy, hs, hr, ag_s, ag_r, one_s, one_r, sf, rf, sb, rb,
    store_y, store_dx, st_s, st_r, ga_s, ga_r, hid_l, hid_s, hid_r,
):
    me = Place()
    k = me.ctx
    pieces = lax.axis_size("ctx")
    last = pieces - 1
    tokens = proj_ref.shape[0]
    half = tokens // 2
    chunks = heads // CHUNK
    cols, depth = w_ref.shape
    band, lanes = cols // 2, depth // 4
    right = {"ctx": lax.rem(k + 1, pieces)}
    left = {"ctx": lax.rem(k + pieces - 1, pieces)}

    barrier = pltpu.get_barrier_semaphore()
    peers = [me.sibling()]
    peers += [me.ring("z", d) for d in (1, 2, 3)]
    peers += [me.ring("x", d) for d in (1, 3)]
    peers += [me.piece(a, b) for a, b in OTHERS]
    for peer in peers:
        pl.semaphore_signal(barrier, inc=1, device_id=peer, device_id_type=MESH)

    def load(s):
        return pltpu.make_async_copy(
            h_ref.at[:, me.columns(s, me.core, depth)], h_all.at[s, me.core], load_h.at[s]
        )

    def lend(s):
        return remote(
            h_ref.at[:, me.columns(s, 1 - me.core, depth)], h_all.at[s, me.core],
            hs.at[s], hr.at[s], me.sibling(),
        )

    loop(8, lambda s: load(s).start())
    load_x = pltpu.make_async_copy(x_hbm, x_ref, load_xy.at[0])
    load_dy = pltpu.make_async_copy(dy_hbm, dy_ref, load_xy.at[1])
    for a in range(2):
        for b in range(4):
            @pl.when((me.x_hi == a) & (me.y == b))
            def _():
                w_all[me.x_lo, me.z, b, a] = w_ref[
                    a * band : (a + 1) * band, b * lanes : (b + 1) * lanes
                ]
    part[...] = jnp.zeros_like(part)
    pl.semaphore_wait(barrier, len(peers))
    loop(8, lambda s: lend(s).start())
    load_x.start()
    load_dy.start()

    @pl.when(k == 0)
    def _():
        state_in[...] = jnp.zeros_like(state_in)

    @pl.when(k == last)
    def _():
        grad_in[...] = jnp.zeros_like(grad_in)

    dq[...] = jnp.zeros_like(dq)
    dk[...] = jnp.zeros_like(dk)
    dscores[...] = jnp.zeros_like(dscores)
    acc_diff[...] = jnp.zeros_like(acc_diff)
    acc_cross[...] = jnp.zeros_like(acc_cross)
    acc_const[...] = jnp.zeros_like(acc_const)

    pending = gather_weights(me, w_ref, w_all, ag_s, ag_r)

    def weights(s):
        parts = [w_all[s // 4, lax.rem(s, 4), b].reshape(cols, lanes) for b in range(4)]
        return jnp.concatenate(parts, axis=1)

    def project(s):
        load(s).wait()
        lend(s).wait_recv()
        part[:, :cols] += dot(h_all[s].reshape(2 * tokens, depth), weights(s), NT)

    loop(8, project)
    mine = pl.ds(pl.multiple_of(me.core * tokens, tokens), tokens)
    theirs = pl.ds(pl.multiple_of((1 - me.core) * tokens, tokens), tokens)
    give = remote(part.at[theirs], proj_in, one_s.at[0], one_r.at[0], me.sibling())
    give.start()
    give.wait_recv()
    pending.append(give)
    proj_ref[...] = part[mine] + proj_in[...]

    rows = lax.broadcasted_iota(jnp.int32, (tokens, tokens), 0)
    columns_at = lax.broadcasted_iota(jnp.int32, (tokens, tokens), 1)
    key = proj_ref[:, :NS]
    query = proj_ref[:, NS : 2 * NS] * NS ** (-0.5)
    pre = proj_ref[:, 2 * NS :] + head_ref[0:1, :]
    rate = jnp.exp(head_ref[1:2, :])
    steps = jnp.maximum(pre, 0.0) + jnp.log1p(jnp.exp(-jnp.abs(pre)))
    running = dot_high((rows >= columns_at).astype(f32), -rate * steps)
    run[...] = running
    run_t[...] = running.T
    step_c[...] = steps
    step_t[...] = steps.T
    key_t[...] = key.T
    query_t[...] = query.T
    high, low_part = split(key)
    key_hl[:, :NS] = high
    key_hl[:, NS:] = low_part
    high, low_part = split(query)
    query_hl[:, :NS] = high
    query_hl[:, NS:] = low_part
    scores[...] = dot_high(query, key, NT)
    load_x.wait()
    load_dy.wait()

    def copy_fwd(j):
        chunk = pl.ds(j * CHUNK, CHUNK)
        return remote(state_out.at[chunk], state_in.at[chunk], sf.at[j], rf.at[j], right)

    def copy_bwd(j):
        chunk = pl.ds(j * CHUNK, CHUNK)
        return remote(grad_out.at[chunk], grad_in.at[chunk], sb.at[j], rb.at[j], left)

    def columns(h, count=1):
        return pl.ds(pl.multiple_of(h * PS, PS), count * PS)

    def forward(j):
        local = []
        for u in range(CHUNK):
            h = j * CHUNK + u
            r_row = run_t[pl.ds(h, 1), :]
            r_end = r_row[:, tokens - 1 : tokens]
            weight = jnp.exp(r_end - r_row) * step_t[pl.ds(h, 1), :]
            high, low_part = split(key_t[...] * weight)
            x = x_ref[:, columns(h)]
            local.append((h, jnp.exp(r_end), dot(high, x) + dot(low_part, x)))

        @pl.when(k > 0)
        def _():
            copy_fwd(j).wait_recv()

        @pl.when(k < last)
        def _():
            for h, decay, state in local:
                state_out[h] = (decay * state_in[h].astype(f32) + state).astype(bf16)
            copy_fwd(j).start()

    def backward(j):
        local = []
        for u in range(CHUNK):
            h = j * CHUNK + u
            r_row = run_t[pl.ds(h, 1), :]
            r_end = r_row[:, tokens - 1 : tokens]
            high, low_part = split(query_t[...] * jnp.exp(r_row))
            dy = dy_ref[:, columns(h)]
            local.append((h, jnp.exp(r_end), dot(high, dy) + dot(low_part, dy)))

        @pl.when(k < last)
        def _():
            copy_bwd(j).wait_recv()

        @pl.when(k > 0)
        def _():
            for h, decay, state in local:
                grad_out[h] = (decay * grad_in[h].astype(f32) + state).astype(bf16)
            copy_bwd(j).start()

    def one_head(h):
        lane = lax.broadcasted_iota(jnp.int32, (tokens, NS), 1)
        at_h = lane == h
        r_col = jnp.sum(jnp.where(at_h, run[...], 0.0), axis=1, keepdims=True)
        s_col = jnp.sum(jnp.where(at_h, step_c[...], 0.0), axis=1, keepdims=True)
        r_row = run_t[pl.ds(h, 1), :]
        s_row = step_t[pl.ds(h, 1), :]
        r_end = r_row[:, tokens - 1 : tokens]
        x = x_ref[:, columns(h)]
        dy = dy_ref[:, columns(h)]
        gain = gain_ref[h]

        def decays(begin, width):
            t = lax.broadcasted_iota(jnp.int32, (half, width), 0) + begin
            s = lax.broadcasted_iota(jnp.int32, (half, width), 1)
            gaps = r_col[begin : begin + half] - r_row[:, :width]
            return jnp.exp(jnp.where(t >= s, gaps, -1e30)) * s_row[:, :width]

        top = decays(0, half)
        bottom = decays(half, tokens)
        mix_top = (top * scores[:half, :half]).astype(bf16)
        mix_bottom = (bottom * scores[half:, :]).astype(bf16)
        ds_top = top * dot(dy[:half], x[:half], NT)
        ds_bottom = bottom * dot(dy[half:], x, NT)
        y = jnp.concatenate([dot(mix_top, x[:half]), dot(mix_bottom, x)], axis=0)
        dx = dot(mix_bottom, dy[half:], TN)
        dx = jnp.concatenate([dx[:half] + dot(mix_top, dy[:half], TN), dx[half:]], axis=0)

        state = state_in[h]
        grad = grad_in[h]
        from_start = jnp.exp(r_col)
        to_end = jnp.exp(r_end - r_col) * s_col
        y += from_start * dot(query_hl[...], jnp.concatenate([state, state], axis=0))
        carried = to_end * dot(key_hl[...], jnp.concatenate([grad, grad], axis=0))
        dx += carried
        dq_h = from_start * dot(dy, state, NT)
        dk_h = to_end * dot(x, grad, NT)
        xf = x.astype(f32)
        dyf = dy.astype(f32)
        y_out = (y + gain * xf).astype(bf16)
        dx_out = (dx + gain * dyf).astype(bf16)
        cross = xf * dx
        cross_h = jnp.sum(cross, axis=1, keepdims=True)
        diff_h = jnp.sum(dyf * y - cross, axis=1, keepdims=True)
        inner = jnp.sum(grad.astype(f32) * state.astype(f32), axis=0, keepdims=True)
        inner = jnp.sum(inner, axis=1, keepdims=True)
        outer = jnp.sum(jnp.sum(xf * carried, axis=0, keepdims=True), axis=1, keepdims=True)
        const_h = jnp.exp(r_end) * inner + outer
        return at_h, ds_top, ds_bottom, dq_h, dk_h, y_out, dx_out, cross_h, diff_h, const_h

    def keep_y(j):
        at = columns(j * CHUNK, CHUNK)
        return pltpu.make_async_copy(x_ref.at[:, at], y_hbm.at[:, at], store_y.at[j])

    def keep_dx(j):
        at = columns(j * CHUNK, CHUNK)
        return pltpu.make_async_copy(dy_ref.at[:, at], dx_hbm.at[:, at], store_dx.at[j])

    def compute(j):
        done = [one_head(j * CHUNK + u) for u in range(CHUNK)]
        ats, ds_tops, ds_bottoms, dqs, dks, ys, dxs, crosses, diffs, consts = zip(*done)
        dscores[:half, :half] += sum(ds_tops[1:], ds_tops[0])
        dscores[half:, :] += sum(ds_bottoms[1:], ds_bottoms[0])
        dq[...] += sum(dqs[1:], dqs[0])
        dk[...] += sum(dks[1:], dks[0])
        cross, diff, const = acc_cross[...], acc_diff[...], acc_const[...]
        for u in range(CHUNK):
            cross = jnp.where(ats[u], crosses[u], cross)
            diff = jnp.where(ats[u], diffs[u], diff)
            const = jnp.where(ats[u][:8], consts[u], const)
        acc_cross[...] = cross
        acc_diff[...] = diff
        acc_const[...] = const
        for u in range(CHUNK):
            x_ref[:, columns(j * CHUNK + u)] = ys[u]
            dy_ref[:, columns(j * CHUNK + u)] = dxs[u]
        keep_y(j).start()
        keep_dx(j).start()

    extra = LAG_FAR - LAG
    start_f = LAG * k + extra * (k // 4)
    start_b = LAG * (last - k) + extra * ((last - k) // 4)
    start_c = jnp.maximum(start_f, start_b)

    def iteration(i):
        jf = i - start_f
        jb = i - start_b
        jc = i - start_c

        @pl.when((jf >= 0) & (jf < chunks))
        def _():
            forward(jf)

        @pl.when((jb >= 0) & (jb < chunks))
        def _():
            backward(jb)

        @pl.when((jc >= 0) & (jc < chunks))
        def _():
            compute(jc)

    loop(chunks + LAG * last + extra, iteration)

    key = proj_ref[:, :NS]
    query = proj_ref[:, NS : 2 * NS] * NS ** (-0.5)
    pre = proj_ref[:, 2 * NS :] + head_ref[0:1, :]
    d_log = dot_high((columns_at >= rows).astype(f32), acc_diff[...]) + acc_const[0:1, :]
    slope = 1.0 / (1.0 + jnp.exp(-pre))
    ratio = jnp.where(pre < -20.0, 1.0, slope / step_c[...])
    dk_all = dk[...] + dot_high(dscores[...].T, query)
    dq_all = (dq[...] + dot_high(dscores[...], key)) * NS ** (-0.5)
    dz_all = acc_cross[...] * ratio - rate * d_log * slope
    g_mine = g_all.at[me.core]
    gt_mine = gt_all.at[me.core]
    for n, grads in enumerate((dk_all, dq_all, dz_all)):
        g_mine[:, n * NS : (n + 1) * NS] = grads.astype(bf16)
        gt_mine[n * NS : (n + 1) * NS, :] = grads.T.astype(bf16)
    give_t = remote(gt_mine, gt_mine, one_s.at[1], one_r.at[1], me.sibling())
    give_g = remote(g_mine, g_mine, one_s.at[2], one_r.at[2], me.sibling())
    give_t.start()
    give_g.start()
    pending += [give_t, give_g]
    give_t.wait_recv()

    def weight_grad(s):
        both = jnp.concatenate([gt_all[0, :cols], gt_all[1, :cols]], axis=1)
        p = dot(both, h_all[s].reshape(2 * tokens, depth))
        for b in range(4):
            for a in range(2):
                block = p[a * band : (a + 1) * band, b * lanes : (b + 1) * lanes]
                own[s // 4, lax.rem(s, 4), b, a] = block
                low[s // 4, lax.rem(s, 4), b, a] = block.astype(bf16)

    loop(8, weight_grad)
    slots = (
        (slot_a0, slot_b0, slot_c0), (slot_a1, slot_b1, slot_c1), (slot_a2, slot_b2, slot_c2)
    )
    current = sum_start(me, low, slots, st_s, st_r)
    give_g.wait_recv()

    def keep_hid(s):
        return pltpu.make_async_copy(
            hid.at[s, me.core], hid_hbm.at[:, me.columns(s, me.core, depth)], hid_l.at[s]
        )

    def give_hid(s):
        return remote(
            hid.at[s, 1 - me.core], hid_hbm.at[:, me.columns(s, me.core, depth)],
            hid_s.at[s], hid_r.at[s], me.sibling(),
        )

    def hidden(s):
        both = g_all[...].reshape(2 * tokens, 3 * NS)
        out = dot(both[:, :cols], weights(s)).astype(bf16)
        hid[s] = out.reshape(2, tokens, depth)
        keep_hid(s).start()
        give_hid(s).start()

    loop(8, hidden)
    pending += sum_finish(
        me, current, own, slots, (sum_a0, sum_a1, sum_a2), (low_a0, low_a1, low_a2),
        (sum_b0, sum_b1, sum_b2), final, gathered, gw_ref, st_s, st_r, ga_s, ga_r,
    )
    for copy in pending:
        copy.wait_send()

    def finish(s):
        lend(s).wait_send()
        keep_hid(s).wait()
        give_hid(s).wait_send()
        give_hid(s).wait_recv()

    loop(8, finish)

    def stored(j):
        keep_y(j).wait()
        keep_dx(j).wait()

    loop(chunks, stored)

    @pl.when(k < last)
    def _():
        loop(chunks, lambda j: copy_fwd(j).wait_send())

    @pl.when(k > 0)
    def _():
        loop(chunks, lambda j: copy_bwd(j).wait_send())


def layer(gain, head, weight_t, h, x, dy):
    tokens, width = x.shape
    heads = width // PS
    chunks = heads // CHUNK
    cols, depth = weight_t.shape
    half, lanes = cols // 2, depth // 4
    sizes = [size for _, size in bands(half)]
    vm = pl.BlockSpec(memory_space=pltpu.VMEM)
    hbm = pl.BlockSpec(memory_space=pl.ANY)
    states = pltpu.VMEM((heads, NS, PS), bf16)
    by_token = pltpu.VMEM((tokens, NS), f32)
    by_state = pltpu.VMEM((NS, tokens), f32)
    square = pltpu.VMEM((tokens, tokens), f32)
    two_parts = pltpu.VMEM((tokens, 2 * NS), bf16)

    def shape(left, color):
        dims = {"x_lo": 2, "z": 4, "y": 4, "x_hi": 2}
        return tuple(n for name, n in dims.items() if name[0] in left) + (sizes[color], lanes)

    def sem(n):
        return pltpu.SemaphoreType.DMA((n,))

    everyone = range(BANDS)
    one = [shape(ORDER_SUM[c][1:], c) for c in everyone]
    two = [shape(ORDER_SUM[c][2:], c) for c in everyone]
    end = [shape("", c) for c in everyone]
    whole = (2, 4, 4, 2, half, lanes)
    return pl.pallas_call(
        partial(layer_kernel, heads),
        out_shape=(
            jax.ShapeDtypeStruct(x.shape, bf16),
            jax.ShapeDtypeStruct(x.shape, bf16),
            jax.ShapeDtypeStruct(h.shape, bf16),
            jax.ShapeDtypeStruct((cols, depth), f32),
        ),
        in_specs=[pl.BlockSpec(memory_space=pltpu.SMEM), vm, vm, hbm, hbm, hbm],
        out_specs=(hbm, hbm, hbm, vm),
        scratch_shapes=[
            pltpu.VMEM((8, 2, tokens, depth), bf16),
            pltpu.VMEM(whole, bf16),
            pltpu.VMEM(x.shape, bf16),
            pltpu.VMEM(x.shape, bf16),
            pltpu.VMEM((2 * tokens, 3 * NS), f32),
            pltpu.VMEM((tokens, 3 * NS), f32),
            pltpu.VMEM((tokens, 3 * NS), f32),
            by_token, by_state, by_state, by_token, by_state, by_state,
            two_parts, two_parts, square,
            by_token, by_token, pltpu.VMEM((8, NS), f32), by_token, by_token, square,
            states, states, states, states,
            pltpu.VMEM((2, tokens, 3 * NS), bf16),
            pltpu.VMEM((2, 3 * NS, tokens), bf16),
            pltpu.VMEM(whole, f32),
            pltpu.VMEM(whole, bf16),
        ]
        + [pltpu.VMEM((3,) + s, bf16) for s in one]
        + [pltpu.VMEM(s, f32) for s in one]
        + [pltpu.VMEM(s, bf16) for s in one]
        + [pltpu.VMEM((3,) + s, bf16) for s in two]
        + [pltpu.VMEM(s, f32) for s in two]
        + [pltpu.VMEM((3,) + s, f32) for s in end]
        + [
            pltpu.VMEM((half, lanes), f32),
            pltpu.VMEM((2, 4, half, lanes), f32),
            pltpu.VMEM((8, 2, tokens, depth), bf16),
            sem(8), sem(2), sem(8), sem(8), sem(27), sem(27), sem(3), sem(3),
            sem(chunks), sem(chunks), sem(chunks), sem(chunks), sem(chunks), sem(chunks),
            sem(27), sem(27), sem(21), sem(21), sem(8), sem(8), sem(8),
        ],
        compiler_params=pltpu.CompilerParams(
            collective_id=0, has_side_effects=True, vmem_limit_bytes=58 * 2**20
        ),
    )(gain, head, weight_t, h, x, dy)


def shards(hidden_rows, inner_rows, weight_proj, decay_log, step_bias, skip_gain, grad_output):
    token_rows = hidden_rows.reshape(-1, hidden_rows.shape[-1])
    value_rows = inner_rows.reshape(-1, inner_rows.shape[-1])
    cotangent = grad_output.reshape(value_rows.shape)
    heads = decay_log.shape[0]
    head = jnp.pad(jnp.stack([step_bias, decay_log]), ((0, 6), (0, NS - heads)))
    output, grad_values, grad_tokens, grad_weight_t = layer(
        skip_gain, head, weight_proj.T, token_rows, value_rows, cotangent
    )
    return (
        output.reshape(inner_rows.shape),
        grad_values.reshape(inner_rows.shape),
        grad_tokens.reshape(hidden_rows.shape),
        grad_weight_t.T,
    )


def solution(mesh):
    rows = P("dp", "ctx", None)
    return jax.shard_map(
        shards,
        mesh=mesh,
        in_specs=(rows, rows, P("dp", None), P(), P(), P(), rows),
        out_specs=(rows, rows, rows, P("dp", None)),
        check_vma=False,
    )
```

time: 359 us -> 170 us (0.47)
  waiting for transfers between devices: 201 us -> 0 us
  Pallas kernels: 114 us -> 157 us
  matrix products: 18.5 us -> 0 us
  between operations: 13.8 us -> 0.65 us
    psum x1 -> x0, waiting for transfers between devices: 80.6 us -> none  [shards(): grad_weight = lax.psum(grad_shard, 'ctx')]
    reduce_scatter x1 -> x0, waiting for transfers between devices: 76.9 us -> none  [shards(): lax.psum_scatter(dot(token_rows, grad_low, TN), 'dp', scatter_dimension=0...]
    all_gather x1 -> x0, waiting for transfers between devices: 42.9 us -> none  [shards(): whole = lax.all_gather(weight_proj, 'dp', axis=0, tiled=True)]
    pallas_call x1, Pallas kernels: 114 us -> 157 us  [layer(): pl.pallas_call(partial(layer_kernel, heads), out_shape=(jax.ShapeDtypeStr...]
    dot_general x3 -> x0, matrix products: 18.5 us -> none  [the longest x2 12.4 us: dot(): return lax.dot_general(a, b, dims, preferred_element_type=f32)]
    unnamed x13 -> x10, local copies, waits for them, and re-layouts: 9.66 us -> 11.3 us
  transfers between devices with their start and end apart: 3 -> 0, of which waited for: 3 -> 0; matrix products, arithmetic and copies ran while one was open for 2% -> 0% of each run, Pallas kernels for 0% -> 0%
where the time goes in v4:
time: 170 us
  Pallas kernels  157 us (92%)
  local copies, waits for them, and re-layouts  11.3 us (7%)
    pallas_call x1, Pallas kernels, layer(): pl.pallas_call(partial(layer_kernel, heads), out_shape=(jax.ShapeDtypeStr...  157 us
    unnamed x10, local copies, waits for them, and re-layouts  11.3 us

profile of v4, /device:TPU:0, one launch (start us, length us, event | category | flops | bytes accessed | tf_op | source)
XLA Modules:
  0.0 169.9 jit_solution(1938985338313755126)
XLA Ops:
  0.6 1.3 select_maximum_fusion.head_ref
  1.9 156.6 %shard_map.102 = (bf16[256,8192]{1,0:T(8,128)(2,1)}, bf16[256,8192]{1,0:T(8,128)(2,1)}, bf16[256,8192]{1,0:T(8,128)(2,1)}, f32[320,512]{1,0:T(8,128)}) custom-call(f32[64]{0:T(128)} %gain_ref.1, f32[8,128]{1,0:T(8,128)} %select_maximum_fusion.head_ref, bf16[320,512]{1,0:T(8,128)(2,1)} %bitcast.17, bf16[256,8192]{1,0:T(8,128)(2,1)} %bitcast.10, ...), custom_call_target="tpu_custom_call" | custom-call | tf_op jit(solution)/shard_map/pallas_call | solution.py:599
  158.5 0.0 copy-start.1
  158.5 4.8 %copy.15 = bf16[1,256,8192]{2,1,0:T(8,128)(2,1)} copy(bf16[1,256,8192]{2,1,0:T(8,128)(2,1)} %bitcast.15) | data formatting | bytes 8388608
  163.3 0.0 copy-done.1
  163.3 0.0 copy-start
  163.3 2.1 %copy.16 = bf16[1,256,8192]{2,1,0:T(8,128)(2,1)} copy(bf16[1,256,8192]{2,1,0:T(8,128)(2,1)S(1)} %bitcast.14) | data formatting | bytes 8388608
  165.5 1.6 copy-done
  167.0 0.0 copy-start.2
  167.0 2.0 %copy.17 = bf16[1,256,8192]{2,1,0:T(8,128)(2,1)} copy(bf16[1,256,8192]{2,1,0:T(8,128)(2,1)S(1)} %bitcast.13) | data formatting | bytes 8388608
  169.0 0.0 copy-done.2
  169.0 0.8 copy.18
Async XLA Ops:
  158.5 4.8 %copy-start.1 = (bf16[256,8192]{1,0:T(8,128)(2,1)S(1)}, bf16[256,8192]{1,0:T(8,128)(2,1)}, u32[]{:S(2)}) copy-start(bf16[256,8192]{1,0:T(8,128)(2,1)} %get-tuple-element.9) | copy-start | bytes 12582916
  163.3 3.7 %copy-start = (bf16[256,8192]{1,0:T(8,128)(2,1)S(1)}, bf16[256,8192]{1,0:T(8,128)(2,1)}, u32[]{:S(2)}) copy-start(bf16[256,8192]{1,0:T(8,128)(2,1)} %get-tuple-element.10) | copy-start | bytes 12582916
  167.0 2.0 %copy-start.2 = (f32[320,512]{1,0:T(8,128)S(1)}, f32[320,512]{1,0:T(8,128)}, u32[]{:S(2)}) copy-start(f32[320,512]{1,0:T(8,128)} %get-tuple-element.11) | copy-start | bytes 1966084

commit v5 on v4

--- a/solution.py
+++ b/solution.py
@@ -188,7 +188,8 @@
     gathers = []
     for color in range(BANDS):
         off, size = bands(half)[color]
-        final[pl.ds(off, size)] = arrived(color, 2, finals[color], ORDER_SUM[color][2:])
+        total = arrived(color, 2, finals[color], ORDER_SUM[color][2:])
+        final[pl.ds(off, size)] = total.astype(bf16)
         for m, (a, b) in enumerate(OTHERS):
             n = color * 7 + m
             gathers.append(
@@ -203,24 +204,24 @@
     for a in range(2):
         for b in range(4):
             mine = (me.x_hi == a) & (me.y == b)
-            part = jnp.where(mine, final[...], gathered[a, b])
+            part = jnp.where(mine, final[...].astype(f32), gathered[a, b].astype(f32))
             out_ref[a * half : (a + 1) * half, b * lanes : (b + 1) * lanes] = part
     return pending + gathers
 
 
 def layer_kernel(
-    heads, gain_ref, head_ref, w_ref, h_ref, x_hbm, dy_hbm,
-    y_hbm, dx_hbm, hid_hbm, gw_ref,
-    h_all, w_all, x_ref, dy_ref, part, proj_in, proj_ref,
+    heads, gain_ref, decay_ref, bias_ref, w_ref, h_ref, x_hbm, dy_hbm,
+    x_ref, dy_ref, hid_ref, gw_ref,
+    h_all, w_all, part, proj_in, proj_ref,
     run, run_t, step_t, step_c, key_t, query_t, key_hl, query_hl, scores,
     acc_diff, acc_cross, acc_const, dq, dk, dscores,
-    state_in, state_out, grad_in, grad_out,
+    state_in, state_out, grad_in, grad_out, state_own, grad_own,
     g_all, gt_all, own, low,
     slot_a0, slot_a1, slot_a2, sum_a0, sum_a1, sum_a2, low_a0, low_a1, low_a2,
     slot_b0, slot_b1, slot_b2, sum_b0, sum_b1, sum_b2,
     slot_c0, slot_c1, slot_c2, final, gathered, hid,
     load_h, load_xy, hs, hr, ag_s, ag_r, one_s, one_r, sf, rf, sb, rb,
-    store_y, store_dx, st_s, st_r, ga_s, ga_r, hid_l, hid_s, hid_r,
+    st_s, st_r, ga_s, ga_r, hid_s, hid_r,
 ):
     me = Place()
     k = me.ctx
@@ -233,6 +234,9 @@
     band, lanes = cols // 2, depth // 4
     right = {"ctx": lax.rem(k + 1, pieces)}
     left = {"ctx": lax.rem(k + pieces - 1, pieces)}
+
+    def widened(ref):
+        return jnp.concatenate([ref[...], jnp.zeros((1, NS - heads), f32)], axis=1)
 
     barrier = pltpu.get_barrier_semaphore()
     peers = [me.sibling()]
@@ -308,8 +312,8 @@
     columns_at = lax.broadcasted_iota(jnp.int32, (tokens, tokens), 1)
     key = proj_ref[:, :NS]
     query = proj_ref[:, NS : 2 * NS] * NS ** (-0.5)
-    pre = proj_ref[:, 2 * NS :] + head_ref[0:1, :]
-    rate = jnp.exp(head_ref[1:2, :])
+    pre = proj_ref[:, 2 * NS :] + widened(bias_ref)
+    rate = jnp.exp(widened(decay_ref))
     steps = jnp.maximum(pre, 0.0) + jnp.log1p(jnp.exp(-jnp.abs(pre)))
     running = dot_high((rows >= columns_at).astype(f32), -rate * steps)
     run[...] = running
@@ -328,57 +332,61 @@
     load_x.wait()
     load_dy.wait()
 
-    def copy_fwd(j):
-        chunk = pl.ds(j * CHUNK, CHUNK)
-        return remote(state_out.at[chunk], state_in.at[chunk], sf.at[j], rf.at[j], right)
-
-    def copy_bwd(j):
-        chunk = pl.ds(j * CHUNK, CHUNK)
-        return remote(grad_out.at[chunk], grad_in.at[chunk], sb.at[j], rb.at[j], left)
+    def copy_fwd(h):
+        return remote(state_out.at[h], state_in.at[h], sf.at[h], rf.at[h], right)
+
+    def copy_bwd(h):
+        return remote(grad_out.at[h], grad_in.at[h], sb.at[h], rb.at[h], left)
 
     def columns(h, count=1):
         return pl.ds(pl.multiple_of(h * PS, PS), count * PS)
 
-    def forward(j):
-        local = []
+    def prepare(j):
+        made = []
         for u in range(CHUNK):
             h = j * CHUNK + u
             r_row = run_t[pl.ds(h, 1), :]
             r_end = r_row[:, tokens - 1 : tokens]
-            weight = jnp.exp(r_end - r_row) * step_t[pl.ds(h, 1), :]
-            high, low_part = split(key_t[...] * weight)
+            high, low_part = split(key_t[...] * (jnp.exp(r_end - r_row) * step_t[pl.ds(h, 1), :]))
             x = x_ref[:, columns(h)]
-            local.append((h, jnp.exp(r_end), dot(high, x) + dot(low_part, x)))
-
-        @pl.when(k > 0)
-        def _():
-            copy_fwd(j).wait_recv()
-
-        @pl.when(k < last)
-        def _():
-            for h, decay, state in local:
-                state_out[h] = (decay * state_in[h].astype(f32) + state).astype(bf16)
-            copy_fwd(j).start()
-
-    def backward(j):
-        local = []
+            state = dot(high, x) + dot(low_part, x)
+            high, low_part = split(query_t[...] * jnp.exp(r_row))
+            dy = dy_ref[:, columns(h)]
+            made.append((h, state, dot(high, dy) + dot(low_part, dy)))
+        for h, state, grad in made:
+            state_own[h] = state
+            grad_own[h] = grad
+
+    def decay_of(h):
+        return jnp.exp(run_t[pl.ds(h, 1), :][:, tokens - 1 : tokens])
+
+    def forward(j):
         for u in range(CHUNK):
             h = j * CHUNK + u
-            r_row = run_t[pl.ds(h, 1), :]
-            r_end = r_row[:, tokens - 1 : tokens]
-            high, low_part = split(query_t[...] * jnp.exp(r_row))
-            dy = dy_ref[:, columns(h)]
-            local.append((h, jnp.exp(r_end), dot(high, dy) + dot(low_part, dy)))
-
-        @pl.when(k < last)
-        def _():
-            copy_bwd(j).wait_recv()
-
-        @pl.when(k > 0)
-        def _():
-            for h, decay, state in local:
-                grad_out[h] = (decay * grad_in[h].astype(f32) + state).astype(bf16)
-            copy_bwd(j).start()
+
+            @pl.when(k > 0)
+            def _():
+                copy_fwd(h).wait_recv()
+
+            @pl.when(k < last)
+            def _():
+                carried = decay_of(h) * state_in[h].astype(f32)
+                state_out[h] = (carried + state_own[h]).astype(bf16)
+                copy_fwd(h).start()
+
+    def backward(j):
+        for u in range(CHUNK):
+            h = j * CHUNK + u
+
+            @pl.when(k < last)
+            def _():
+                copy_bwd(h).wait_recv()
+
+            @pl.when(k > 0)
+            def _():
+                carried = decay_of(h) * grad_in[h].astype(f32)
+                grad_out[h] = (carried + grad_own[h]).astype(bf16)
+                copy_bwd(h).start()
 
     def one_head(h):
         lane = lax.broadcasted_iota(jnp.int32, (tokens, NS), 1)
@@ -430,14 +438,6 @@
         const_h = jnp.exp(r_end) * inner + outer
         return at_h, ds_top, ds_bottom, dq_h, dk_h, y_out, dx_out, cross_h, diff_h, const_h
 
-    def keep_y(j):
-        at = columns(j * CHUNK, CHUNK)
-        return pltpu.make_async_copy(x_ref.at[:, at], y_hbm.at[:, at], store_y.at[j])
-
-    def keep_dx(j):
-        at = columns(j * CHUNK, CHUNK)
-        return pltpu.make_async_copy(dy_ref.at[:, at], dx_hbm.at[:, at], store_dx.at[j])
-
     def compute(j):
         done = [one_head(j * CHUNK + u) for u in range(CHUNK)]
         ats, ds_tops, ds_bottoms, dqs, dks, ys, dxs, crosses, diffs, consts = zip(*done)
@@ -456,8 +456,6 @@
         for u in range(CHUNK):
             x_ref[:, columns(j * CHUNK + u)] = ys[u]
             dy_ref[:, columns(j * CHUNK + u)] = dxs[u]
-        keep_y(j).start()
-        keep_dx(j).start()
 
     extra = LAG_FAR - LAG
     start_f = LAG * k + extra * (k // 4)
@@ -469,6 +467,10 @@
         jb = i - start_b
         jc = i - start_c
 
+        @pl.when(i < chunks)
+        def _():
+            prepare(i)
+
         @pl.when((jf >= 0) & (jf < chunks))
         def _():
             forward(jf)
@@ -485,7 +487,7 @@
 
     key = proj_ref[:, :NS]
     query = proj_ref[:, NS : 2 * NS] * NS ** (-0.5)
-    pre = proj_ref[:, 2 * NS :] + head_ref[0:1, :]
+    pre = proj_ref[:, 2 * NS :] + widened(bias_ref)
     d_log = dot_high((columns_at >= rows).astype(f32), acc_diff[...]) + acc_const[0:1, :]
     slope = 1.0 / (1.0 + jnp.exp(-pre))
     ratio = jnp.where(pre < -20.0, 1.0, slope / step_c[...])
@@ -502,41 +504,40 @@
     give_t.start()
     give_g.start()
     pending += [give_t, give_g]
-    give_t.wait_recv()
-
-    def weight_grad(s):
-        both = jnp.concatenate([gt_all[0, :cols], gt_all[1, :cols]], axis=1)
-        p = dot(both, h_all[s].reshape(2 * tokens, depth))
+
+    def weight_grad(s, side, more):
+        p = dot(gt_all[side, :cols], h_all[s, side])
         for b in range(4):
             for a in range(2):
+                at = (s // 4, lax.rem(s, 4), b, a)
                 block = p[a * band : (a + 1) * band, b * lanes : (b + 1) * lanes]
-                own[s // 4, lax.rem(s, 4), b, a] = block
-                low[s // 4, lax.rem(s, 4), b, a] = block.astype(bf16)
-
-    loop(8, weight_grad)
+                if more:
+                    block += own[at]
+                    low[at] = block.astype(bf16)
+                own[at] = block
+
+    loop(8, lambda s: weight_grad(s, me.core, False))
+    give_t.wait_recv()
+    loop(8, lambda s: weight_grad(s, 1 - me.core, True))
     slots = (
         (slot_a0, slot_b0, slot_c0), (slot_a1, slot_b1, slot_c1), (slot_a2, slot_b2, slot_c2)
     )
     current = sum_start(me, low, slots, st_s, st_r)
     give_g.wait_recv()
 
-    def keep_hid(s):
-        return pltpu.make_async_copy(
-            hid.at[s, me.core], hid_hbm.at[:, me.columns(s, me.core, depth)], hid_l.at[s]
-        )
-
     def give_hid(s):
         return remote(
-            hid.at[s, 1 - me.core], hid_hbm.at[:, me.columns(s, me.core, depth)],
+            hid.at[s], hid_ref.at[:, me.columns(s, me.core, depth)],
             hid_s.at[s], hid_r.at[s], me.sibling(),
         )
 
     def hidden(s):
-        both = g_all[...].reshape(2 * tokens, 3 * NS)
-        out = dot(both[:, :cols], weights(s)).astype(bf16)
-        hid[s] = out.reshape(2, tokens, depth)
-        keep_hid(s).start()
+        theirs = g_all[1 - me.core]
+        hid[s] = dot(theirs[:, :cols], weights(s)).astype(bf16)
         give_hid(s).start()
+        hid_ref[:, me.columns(s, me.core, depth)] = dot(
+            g_all[me.core, :, :cols], weights(s)
+        ).astype(bf16)
 
     loop(8, hidden)
     pending += sum_finish(
@@ -548,28 +549,21 @@
 
     def finish(s):
         lend(s).wait_send()
-        keep_hid(s).wait()
         give_hid(s).wait_send()
         give_hid(s).wait_recv()
 
     loop(8, finish)
 
-    def stored(j):
-        keep_y(j).wait()
-        keep_dx(j).wait()
-
-    loop(chunks, stored)
-
     @pl.when(k < last)
     def _():
-        loop(chunks, lambda j: copy_fwd(j).wait_send())
+        loop(heads, lambda h: copy_fwd(h).wait_send())
 
     @pl.when(k > 0)
     def _():
-        loop(chunks, lambda j: copy_bwd(j).wait_send())
-
-
-def layer(gain, head, weight_t, h, x, dy):
+        loop(heads, lambda h: copy_bwd(h).wait_send())
+
+
+def layer(gain, decay, bias, weight_t, h, x, dy):
     tokens, width = x.shape
     heads = width // PS
     chunks = heads // CHUNK
@@ -579,6 +573,7 @@
     vm = pl.BlockSpec(memory_space=pltpu.VMEM)
     hbm = pl.BlockSpec(memory_space=pl.ANY)
     states = pltpu.VMEM((heads, NS, PS), bf16)
+    own_states = pltpu.VMEM((heads, NS, PS), f32)
     by_token = pltpu.VMEM((tokens, NS), f32)
     by_state = pltpu.VMEM((NS, tokens), f32)
     square = pltpu.VMEM((tokens, tokens), f32)
@@ -599,25 +594,23 @@
     return pl.pallas_call(
         partial(layer_kernel, heads),
         out_shape=(
-            jax.ShapeDtypeStruct(x.shape, bf16),
-            jax.ShapeDtypeStruct(x.shape, bf16),
-            jax.ShapeDtypeStruct(h.shape, bf16),
-            jax.ShapeDtypeStruct((cols, depth), f32),
+            pltpu.VMEM(x.shape, bf16),
+            pltpu.VMEM(x.shape, bf16),
+            pltpu.VMEM(h.shape, bf16),
+            pltpu.VMEM((cols, depth), f32),
         ),
-        in_specs=[pl.BlockSpec(memory_space=pltpu.SMEM), vm, vm, hbm, hbm, hbm],
-        out_specs=(hbm, hbm, hbm, vm),
+        in_specs=[pl.BlockSpec(memory_space=pltpu.SMEM), vm, vm, vm, hbm, hbm, hbm],
+        out_specs=(vm, vm, vm, vm),
         scratch_shapes=[
             pltpu.VMEM((8, 2, tokens, depth), bf16),
             pltpu.VMEM(whole, bf16),
-            pltpu.VMEM(x.shape, bf16),
-            pltpu.VMEM(x.shape, bf16),
             pltpu.VMEM((2 * tokens, 3 * NS), f32),
             pltpu.VMEM((tokens, 3 * NS), f32),
             pltpu.VMEM((tokens, 3 * NS), f32),
             by_token, by_state, by_state, by_token, by_state, by_state,
             two_parts, two_parts, square,
             by_token, by_token, pltpu.VMEM((8, NS), f32), by_token, by_token, square,
-            states, states, states, states,
+            states, states, states, states, own_states, own_states,
             pltpu.VMEM((2, tokens, 3 * NS), bf16),
             pltpu.VMEM((2, 3 * NS, tokens), bf16),
             pltpu.VMEM(whole, f32),
@@ -630,27 +623,56 @@
         + [pltpu.VMEM(s, f32) for s in two]
         + [pltpu.VMEM((3,) + s, f32) for s in end]
         + [
-            pltpu.VMEM((half, lanes), f32),
-            pltpu.VMEM((2, 4, half, lanes), f32),
-            pltpu.VMEM((8, 2, tokens, depth), bf16),
+            pltpu.VMEM((half, lanes), bf16),
+            pltpu.VMEM((2, 4, half, lanes), bf16),
+            pltpu.VMEM((8, tokens, depth), bf16),
             sem(8), sem(2), sem(8), sem(8), sem(27), sem(27), sem(3), sem(3),
-            sem(chunks), sem(chunks), sem(chunks), sem(chunks), sem(chunks), sem(chunks),
-            sem(27), sem(27), sem(21), sem(21), sem(8), sem(8), sem(8),
+            sem(heads), sem(heads), sem(heads), sem(heads),
+            sem(27), sem(27), sem(21), sem(21), sem(8), sem(8),
         ],
         compiler_params=pltpu.CompilerParams(
-            collective_id=0, has_side_effects=True, vmem_limit_bytes=58 * 2**20
+            collective_id=0, has_side_effects=True, vmem_limit_bytes=46 * 2**20
         ),
-    )(gain, head, weight_t, h, x, dy)
+    )(gain, decay, bias, weight_t, h, x, dy)
+
+
+def store_kernel(*refs):
+    sems = refs[8]
+    copies = []
+    for source, target in zip(refs[:4], refs[4:8]):
+        rows = source.shape[0] // 2
+        for part in range(2):
+            at = pl.ds(part * rows, rows)
+            copies.append(
+                pltpu.make_async_copy(source.at[at], target.at[at], sems.at[len(copies)])
+            )
+            copies[-1].start()
+    for copy in copies:
+        copy.wait()
+
+
+def store(*arrays):
+    hbm = pl.BlockSpec(memory_space=pl.ANY)
+    vm = pl.BlockSpec(memory_space=pltpu.VMEM)
+    return pl.pallas_call(
+        store_kernel,
+        out_shape=tuple(jax.ShapeDtypeStruct(a.shape, a.dtype) for a in arrays),
+        in_specs=[vm] * 4,
+        out_specs=(hbm,) * 4,
+        scratch_shapes=[pltpu.SemaphoreType.DMA((8,))],
+        compiler_params=pltpu.CompilerParams(vmem_limit_bytes=16 * 2**20),
+    )(*arrays)
 
 
 def shards(hidden_rows, inner_rows, weight_proj, decay_log, step_bias, skip_gain, grad_output):
     token_rows = hidden_rows.reshape(-1, hidden_rows.shape[-1])
     value_rows = inner_rows.reshape(-1, inner_rows.shape[-1])
     cotangent = grad_output.reshape(value_rows.shape)
-    heads = decay_log.shape[0]
-    head = jnp.pad(jnp.stack([step_bias, decay_log]), ((0, 6), (0, NS - heads)))
     output, grad_values, grad_tokens, grad_weight_t = layer(
-        skip_gain, head, weight_proj.T, token_rows, value_rows, cotangent
+        skip_gain, decay_log[None], step_bias[None], weight_proj.T, token_rows, value_rows, cotangent
+    )
+    output, grad_values, grad_tokens, grad_weight_t = store(
+        output, grad_values, grad_tokens, grad_weight_t
     )
     return (
         output.reshape(inner_rows.shape),

time: 170 us -> 161 us (0.947)
  local copies, waits for them, and re-layouts: 11.3 us -> 0 us
  Pallas kernels: 157 us -> 161 us
    unnamed x10 -> x0, local copies, waits for them, and re-layouts: 11.3 us -> none
    pallas_call x1 -> x2, Pallas kernels: 157 us -> 161 us  [the longest x1 156 us: layer(): pl.pallas_call(partial(layer_kernel, heads), out_shape=(pltpu.VMEM(x.shap...]
where the time goes in v5:
time: 161 us
  Pallas kernels  161 us (100%)
    pallas_call x1, Pallas kernels, layer(): pl.pallas_call(partial(layer_kernel, heads), out_shape=(pltpu.VMEM(x.shap...  156 us
    pallas_call x1, Pallas kernels, store(): pl.pallas_call(store_kernel, out_shape=tuple((jax.ShapeDtypeStruct(a.shap...  4.8 us

profile of v5, /device:TPU:0, one launch (start us, length us, event | category | flops | bytes accessed | tf_op | source)
XLA Modules:
  0.0 161.3 jit_solution(5524000989767475159)
XLA Ops:
  0.6 155.8 %shard_map.102 = (bf16[256,8192]{1,0:T(8,128)(2,1)S(1)}, bf16[256,8192]{1,0:T(8,128)(2,1)S(1)}, bf16[256,8192]{1,0:T(8,128)(2,1)S(1)}, f32[320,512]{1,0:T(8,128)S(1)}) custom-call(f32[64]{0:T(128)} %gain_ref.1, f32[1,64]{1,0:T(1,128)} %bitcast.14, f32[1,64]{1,0:T(1,128)} %bitcast.15, bf16[320,512]{1,0:T(8,128)(2,1)} %bitcast.13, bf16[256,8192]{1,0:T(8,128)(2,1)} %bitcast.10, ...), custom_call_target="tpu_custom_call" | custom-call | tf_op jit(solution)/shard_map/pallas_call | solution.py:594
  156.5 4.8 %shard_map.103 = (bf16[256,8192]{1,0:T(8,128)(2,1)}, bf16[256,8192]{1,0:T(8,128)(2,1)}, bf16[256,8192]{1,0:T(8,128)(2,1)}, f32[320,512]{1,0:T(8,128)}) custom-call(bf16[256,8192]{1,0:T(8,128)(2,1)S(1)} %get-tuple-element.12.refs_0_, bf16[256,8192]{1,0:T(8,128)(2,1)S(1)} %get-tuple-element.13.refs_1_, bf16[256,8192]{1,0:T(8,128)(2,1)S(1)} %get-tuple-element.14.refs_2_, ...), custom_call_target="tpu_custom_call" | custom-call | tf_op jit(solution)/shard_map/pallas_call | solution.py:657

commit v6 on v5

--- a/solution.py
+++ b/solution.py
@@ -10,8 +10,8 @@
 PS = 128
 NS = 128
 CHUNK = 2
-LAG = 2
-LAG_FAR = 4
+LAG = 3
+LAG_FAR = 5
 MESH = pl.DeviceIdType.MESH
 highest = lax.Precision.HIGHEST
 f32 = jnp.float32
@@ -40,7 +40,8 @@
 
 def bands(half):
     third = half // 3 // 16 * 16
-    return ((0, third), (third, third), (2 * third, half - 2 * third))
+    first = half - 2 * third
+    return ((0, first), (first, third), (first + third, third))
 
 
 def remote(src, dst, send, recv, device):
@@ -114,7 +115,7 @@
         axis = ORDER_GATHER[color][stage]
         part = region(color, ORDER_GATHER[color][:stage])
         copies = []
-        for d in (1, 3, 2):
+        for d in (2, 1, 3):
             n = color * 9 + stage * 3 + d - 1
             copies.append(remote(part, part, send.at[n], recv.at[n], me.ring(axis, d)))
             copies[-1].start()
@@ -149,7 +150,7 @@
     off, size = bands(slots[0][2].shape[1] + slots[1][2].shape[1] + slots[2][2].shape[1])[color]
     window = (pl.ds(off, size),) if stage == 0 else ()
     copies = []
-    for d in (1, 3, 2):
+    for d in (2, 1, 3):
         n = color * 9 + stage * 3 + d - 1
         part = source.at[pick(left, axis, me.along(axis, d)) + window]
         copies.append(
@@ -294,19 +295,24 @@
         parts = [w_all[s // 4, lax.rem(s, 4), b].reshape(cols, lanes) for b in range(4)]
         return jnp.concatenate(parts, axis=1)
 
-    def project(s):
+    def project(s, side):
+        part[side, :, :cols] += dot(h_all[s, side], weights(s), NT)
+
+    def project_theirs(s):
+        lend(s).wait_recv()
+        project(s, 1 - me.core)
+
+    def project_mine(s):
         load(s).wait()
-        lend(s).wait_recv()
-        part[:, :cols] += dot(h_all[s].reshape(2 * tokens, depth), weights(s), NT)
-
-    loop(8, project)
-    mine = pl.ds(pl.multiple_of(me.core * tokens, tokens), tokens)
-    theirs = pl.ds(pl.multiple_of((1 - me.core) * tokens, tokens), tokens)
-    give = remote(part.at[theirs], proj_in, one_s.at[0], one_r.at[0], me.sibling())
+        project(s, me.core)
+
+    loop(8, project_theirs)
+    give = remote(part.at[1 - me.core], proj_in, one_s.at[0], one_r.at[0], me.sibling())
     give.start()
+    loop(8, project_mine)
     give.wait_recv()
     pending.append(give)
-    proj_ref[...] = part[mine] + proj_in[...]
+    proj_ref[...] = part[me.core] + proj_in[...]
 
     rows = lax.broadcasted_iota(jnp.int32, (tokens, tokens), 0)
     columns_at = lax.broadcasted_iota(jnp.int32, (tokens, tokens), 1)
@@ -460,7 +466,7 @@
     extra = LAG_FAR - LAG
     start_f = LAG * k + extra * (k // 4)
     start_b = LAG * (last - k) + extra * ((last - k) // 4)
-    start_c = jnp.maximum(start_f, start_b)
+    start_c = LAG * last + extra
 
     def iteration(i):
         jf = i - start_f
@@ -604,7 +610,7 @@
         scratch_shapes=[
             pltpu.VMEM((8, 2, tokens, depth), bf16),
             pltpu.VMEM(whole, bf16),
-            pltpu.VMEM((2 * tokens, 3 * NS), f32),
+            pltpu.VMEM((2, tokens, 3 * NS), f32),
             pltpu.VMEM((tokens, 3 * NS), f32),
             pltpu.VMEM((tokens, 3 * NS), f32),
             by_token, by_state, by_state, by_token, by_state, by_state,

time: 161 us -> 157 us (0.975)
  Pallas kernels: 161 us -> 156 us
    pallas_call x1, Pallas kernels: 156 us -> 151 us  [layer(): pl.pallas_call(partial(layer_kernel, heads), out_shape=(pltpu.VMEM(x.shap...]
where the time goes in v6:
time: 157 us
  Pallas kernels  156 us (99%)
    pallas_call x1, Pallas kernels, layer(): pl.pallas_call(partial(layer_kernel, heads), out_shape=(pltpu.VMEM(x.shap...  151 us
    pallas_call x1, Pallas kernels, store(): pl.pallas_call(store_kernel, out_shape=tuple((jax.ShapeDtypeStruct(a.shap...  4.8 us

profile of v6, /device:TPU:0, one launch (start us, length us, event | category | flops | bytes accessed | tf_op | source)
XLA Modules:
  0.0 156.6 jit_solution(5399063039137060783)
XLA Ops:
  0.6 151.2 %shard_map.102 = (bf16[256,8192]{1,0:T(8,128)(2,1)S(1)}, bf16[256,8192]{1,0:T(8,128)(2,1)S(1)}, bf16[256,8192]{1,0:T(8,128)(2,1)S(1)}, f32[320,512]{1,0:T(8,128)S(1)}) custom-call(f32[64]{0:T(128)} %gain_ref.1, f32[1,64]{1,0:T(1,128)} %bitcast.14, f32[1,64]{1,0:T(1,128)} %bitcast.15, bf16[320,512]{1,0:T(8,128)(2,1)} %bitcast.13, bf16[256,8192]{1,0:T(8,128)(2,1)} %bitcast.10, ...), custom_call_target="tpu_custom_call" | custom-call | tf_op jit(solution)/shard_map/pallas_call | solution.py:600
  151.8 4.8 %shard_map.103 = (bf16[256,8192]{1,0:T(8,128)(2,1)}, bf16[256,8192]{1,0:T(8,128)(2,1)}, bf16[256,8192]{1,0:T(8,128)(2,1)}, f32[320,512]{1,0:T(8,128)}) custom-call(bf16[256,8192]{1,0:T(8,128)(2,1)S(1)} %get-tuple-element.12.refs_0_, bf16[256,8192]{1,0:T(8,128)(2,1)S(1)} %get-tuple-element.13.refs_1_, bf16[256,8192]{1,0:T(8,128)(2,1)S(1)} %get-tuple-element.14.refs_2_, ...), custom_call_target="tpu_custom_call" | custom-call | tf_op jit(solution)/shard_map/pallas_call | solution.py:663

commit v7 on v6

--- a/solution.py
+++ b/solution.py
@@ -258,22 +258,19 @@
             hs.at[s], hr.at[s], me.sibling(),
         )
 
-    loop(8, lambda s: load(s).start())
     load_x = pltpu.make_async_copy(x_hbm, x_ref, load_xy.at[0])
     load_dy = pltpu.make_async_copy(dy_hbm, dy_ref, load_xy.at[1])
-    for a in range(2):
-        for b in range(4):
-            @pl.when((me.x_hi == a) & (me.y == b))
-            def _():
-                w_all[me.x_lo, me.z, b, a] = w_ref[
-                    a * band : (a + 1) * band, b * lanes : (b + 1) * lanes
-                ]
+    piece = pltpu.make_async_copy(
+        w_ref.at[
+            pl.ds(pl.multiple_of(me.x_hi * band, 16), band),
+            pl.ds(pl.multiple_of(me.y * lanes, lanes), lanes),
+        ],
+        w_all.at[me.x_lo, me.z, me.y, me.x_hi],
+        load_xy.at[2],
+    )
+    piece.start()
+    loop(8, lambda s: load(s).start())
     part[...] = jnp.zeros_like(part)
-    pl.semaphore_wait(barrier, len(peers))
-    loop(8, lambda s: lend(s).start())
-    load_x.start()
-    load_dy.start()
-
     @pl.when(k == 0)
     def _():
         state_in[...] = jnp.zeros_like(state_in)
@@ -288,6 +285,12 @@
     acc_diff[...] = jnp.zeros_like(acc_diff)
     acc_cross[...] = jnp.zeros_like(acc_cross)
     acc_const[...] = jnp.zeros_like(acc_const)
+
+    piece.wait()
+    pl.semaphore_wait(barrier, len(peers))
+    loop(8, lambda s: lend(s).start())
+    load_x.start()
+    load_dy.start()
 
     pending = gather_weights(me, w_ref, w_all, ag_s, ag_r)
 
@@ -605,7 +608,7 @@
             pltpu.VMEM(h.shape, bf16),
             pltpu.VMEM((cols, depth), f32),
         ),
-        in_specs=[pl.BlockSpec(memory_space=pltpu.SMEM), vm, vm, vm, hbm, hbm, hbm],
+        in_specs=[pl.BlockSpec(memory_space=pltpu.SMEM), vm, vm, hbm, hbm, hbm, hbm],
         out_specs=(vm, vm, vm, vm),
         scratch_shapes=[
             pltpu.VMEM((8, 2, tokens, depth), bf16),
@@ -632,7 +635,7 @@
             pltpu.VMEM((half, lanes), bf16),
             pltpu.VMEM((2, 4, half, lanes), bf16),
             pltpu.VMEM((8, tokens, depth), bf16),
-            sem(8), sem(2), sem(8), sem(8), sem(27), sem(27), sem(3), sem(3),
+            sem(8), sem(3), sem(8), sem(8), sem(27), sem(27), sem(3), sem(3),
             sem(heads), sem(heads), sem(heads), sem(heads),
             sem(27), sem(27), sem(21), sem(21), sem(8), sem(8),
         ],
@@ -646,8 +649,8 @@
     sems = refs[8]
     copies = []
     for source, target in zip(refs[:4], refs[4:8]):
-        rows = source.shape[0] // 2
-        for part in range(2):
+        rows = source.shape[0] // 4
+        for part in range(4):
             at = pl.ds(part * rows, rows)
             copies.append(
                 pltpu.make_async_copy(source.at[at], target.at[at], sems.at[len(copies)])
@@ -665,7 +668,7 @@
         out_shape=tuple(jax.ShapeDtypeStruct(a.shape, a.dtype) for a in arrays),
         in_specs=[vm] * 4,
         out_specs=(hbm,) * 4,
-        scratch_shapes=[pltpu.SemaphoreType.DMA((8,))],
+        scratch_shapes=[pltpu.SemaphoreType.DMA((16,))],
         compiler_params=pltpu.CompilerParams(vmem_limit_bytes=16 * 2**20),
     )(*arrays)
 

time: 157 us -> 156 us (level)
  no operation moved by 1% of the time
where the time goes in v7:
time: 156 us
  Pallas kernels  155 us (99%)
    pallas_call x1, Pallas kernels, layer(): pl.pallas_call(partial(layer_kernel, heads), out_shape=(pltpu.VMEM(x.shap...  151 us
    pallas_call x1, Pallas kernels, store(): pl.pallas_call(store_kernel, out_shape=tuple((jax.ShapeDtypeStruct(a.shap...  4.86 us

profile of v7, /device:TPU:0, one launch (start us, length us, event | category | flops | bytes accessed | tf_op | source)
XLA Modules:
  0.0 156.0 jit_solution(8904191030180391258)
XLA Ops:
  0.6 150.5 %shard_map.102 = (bf16[256,8192]{1,0:T(8,128)(2,1)S(1)}, bf16[256,8192]{1,0:T(8,128)(2,1)S(1)}, bf16[256,8192]{1,0:T(8,128)(2,1)S(1)}, f32[320,512]{1,0:T(8,128)S(1)}) custom-call(f32[64]{0:T(128)} %gain_ref.1, f32[1,64]{1,0:T(1,128)} %bitcast.14, f32[1,64]{1,0:T(1,128)} %bitcast.15, bf16[320,512]{1,0:T(8,128)(2,1)} %bitcast.13, bf16[256,8192]{1,0:T(8,128)(2,1)} %bitcast.10, ...), custom_call_target="tpu_custom_call" | custom-call | tf_op jit(solution)/shard_map/pallas_call | solution.py:603
  151.2 4.9 %shard_map.103 = (bf16[256,8192]{1,0:T(8,128)(2,1)}, bf16[256,8192]{1,0:T(8,128)(2,1)}, bf16[256,8192]{1,0:T(8,128)(2,1)}, f32[320,512]{1,0:T(8,128)}) custom-call(bf16[256,8192]{1,0:T(8,128)(2,1)S(1)} %get-tuple-element.12.refs_0_, bf16[256,8192]{1,0:T(8,128)(2,1)S(1)} %get-tuple-element.13.refs_1_, bf16[256,8192]{1,0:T(8,128)(2,1)S(1)} %get-tuple-element.14.refs_2_, ...), custom_call_target="tpu_custom_call" | custom-call | tf_op jit(solution)/shard_map/pallas_call | solution.py:666

commit v8 on v7

--- a/solution.py
+++ b/solution.py
@@ -11,7 +11,7 @@
 NS = 128
 CHUNK = 2
 LAG = 3
-LAG_FAR = 5
+LAG_FAR = 4
 MESH = pl.DeviceIdType.MESH
 highest = lax.Precision.HIGHEST
 f32 = jnp.float32

time: 156 us -> 155 us (level)
  no operation moved by 1% of the time
where the time goes in v8:
time: 155 us
  Pallas kernels  154 us (99%)
    pallas_call x1, Pallas kernels, layer(): pl.pallas_call(partial(layer_kernel, heads), out_shape=(pltpu.VMEM(x.shap...  150 us
    pallas_call x1, Pallas kernels, store(): pl.pallas_call(store_kernel, out_shape=tuple((jax.ShapeDtypeStruct(a.shap...  4.86 us

profile of v8, /device:TPU:0, one launch (start us, length us, event | category | flops | bytes accessed | tf_op | source)
XLA Modules:
  0.0 155.1 jit_solution(12283995364047546427)
XLA Ops:
  0.6 149.6 %shard_map.102 = (bf16[256,8192]{1,0:T(8,128)(2,1)S(1)}, bf16[256,8192]{1,0:T(8,128)(2,1)S(1)}, bf16[256,8192]{1,0:T(8,128)(2,1)S(1)}, f32[320,512]{1,0:T(8,128)S(1)}) custom-call(f32[64]{0:T(128)} %gain_ref.1, f32[1,64]{1,0:T(1,128)} %bitcast.14, f32[1,64]{1,0:T(1,128)} %bitcast.15, bf16[320,512]{1,0:T(8,128)(2,1)} %bitcast.13, bf16[256,8192]{1,0:T(8,128)(2,1)} %bitcast.10, ...), custom_call_target="tpu_custom_call" | custom-call | tf_op jit(solution)/shard_map/pallas_call | solution.py:603
  150.2 4.9 %shard_map.103 = (bf16[256,8192]{1,0:T(8,128)(2,1)}, bf16[256,8192]{1,0:T(8,128)(2,1)}, bf16[256,8192]{1,0:T(8,128)(2,1)}, f32[320,512]{1,0:T(8,128)}) custom-call(bf16[256,8192]{1,0:T(8,128)(2,1)S(1)} %get-tuple-element.12.refs_0_, bf16[256,8192]{1,0:T(8,128)(2,1)S(1)} %get-tuple-element.13.refs_1_, bf16[256,8192]{1,0:T(8,128)(2,1)S(1)} %get-tuple-element.14.refs_2_, ...), custom_call_target="tpu_custom_call" | custom-call | tf_op jit(solution)/shard_map/pallas_call | solution.py:666
